TPU v7x, 32 devices: a whole 2x2x4 slice. The times are simulated.
32 devices in a mesh: xline: 8 (over z, x), iline: 4 (over y, core).
Axes of the slice: x: 2, y: 2, z: 4, core: 2. Of those that a mesh axis runs over, the one named last changes fastest.
Arguments:
- traces: bfloat16 [16384, 1536], P(('xline', 'iline')), may hold values from -16 to 16
- trace_offset: bfloat16 [16384], P(('xline', 'iline')), may hold values from 0 to 1
- trace_owner: int32 [16384], P(('xline', 'iline')), may hold values from 0 to 31, as said below
- trace_cell: int32 [16384], P(('xline', 'iline')), may hold values from 0 to 7
- slowness: float32 [16, 16, 1536], P('xline', 'iline'), may hold values from 1 to 36
- band_start: int32 [1536], replicated, may hold values from 0 to 1528, as said below
- dip_shift: int32 [9, 16, 16], P(None, 'xline', 'iline'), may hold values from -4 to 4
Outputs:
- smoothed: float32 [16, 16, 1536], P('xline', 'iline')
Inputs may be any that keep to these rules, and one draw needn't show every extreme that they name: `trace_owner`: at most 20 traces of one device (one aligned block of 512 rows) share a bin block, and one particular bin block receives exactly 20 traces from every device. band_start[t] - t lies between -(7) and 0 for every t.
All inputs are finite; a program needn't handle non-finite values.
Results may differ from a plain program's by a relative error of at most 0.0003.
Values may be sent and summed in bfloat16 or wider, within the bound.
A program may use at most 64 MiB of HBM per device.

v0:
```python
import jax
import jax.numpy as jnp
from jax import lax
from jax.sharding import PartitionSpec as P

BAND = 8
DIP = 4


CENTER_WEIGHT = 0.5
SIDE_WEIGHT = 0.0625


def with_halo(value, sides, width):
    for axis, dim in sides:
        size, length = (lax.axis_size(axis), value.shape[dim])
        up = [(i, (i + 1) % size) for i in range(size - 1)]
        down = [(j, i) for i, j in up]
        last = lax.slice_in_dim(value, length - width, length, axis=dim)
        initial = lax.slice_in_dim(value, 0, width, axis=dim)
        before = lax.ppermute(last, axis, up)
        after = lax.ppermute(initial, axis, down)
        value = jnp.concatenate([before, value, after], axis=dim)
    return value


def corrected_rows(trace_rows, offset_rows, slow_rows, band_start):
    samples = trace_rows.shape[1]
    reach = BAND - 1
    sample_ints = jnp.arange(samples, dtype=jnp.int32)
    sample_times = sample_ints.astype(jnp.float32)
    moveout = jnp.sqrt(
        sample_times[None, :] * sample_times[None, :]
        + (offset_rows * offset_rows)[:, None] * slow_rows
    )
    lead = band_start - sample_ints
    widened = jnp.pad(trace_rows, ((0, 0), (reach, reach)))
    numerator = jnp.zeros(moveout.shape, jnp.float32)
    denominator = jnp.zeros(moveout.shape, jnp.float32)
    for step_ahead in range(-reach, reach + 1):
        inside = (step_ahead >= lead) & (step_ahead <= lead + reach)
        picked = widened[:, reach + step_ahead : reach + step_ahead + samples].astype(jnp.float32)
        distance = (sample_times + float(step_ahead))[None, :] - moveout
        weight = jnp.where(inside[None, :], 1.0 / (1.0 + distance * distance), 0.0)
        numerator = numerator + weight * picked
        denominator = denominator + weight
    return numerator / denominator


def smooth_bins(padded, dip_shift, rows_x, rows_y):
    samples = padded.shape[2]
    result = jnp.zeros((rows_x, rows_y, samples), jnp.float32)
    for neighbour in range(9):
        shift_x = neighbour // 3
        shift_y = neighbour % 3
        window = padded[shift_x : shift_x + rows_x, shift_y : shift_y + rows_y, :]
        widened = jnp.pad(window, ((0, 0), (0, 0), (DIP, DIP)))
        shifted = jnp.zeros((rows_x, rows_y, samples), jnp.float32)
        for lag in range(-DIP, DIP + 1):
            chosen = (dip_shift[neighbour] == lag)[:, :, None]
            shifted = shifted + jnp.where(
                chosen, widened[:, :, DIP + lag : DIP + lag + samples], 0.0
            )
        factor = CENTER_WEIGHT if neighbour == 4 else SIDE_WEIGHT
        result = result + factor * shifted
    return result


def body(traces, trace_offset, trace_owner, trace_cell, slowness, band_start, dip_shift):
    owners = lax.axis_size(("xline", "iline"))
    row_count = traces.shape[0]
    samples = traces.shape[1]
    capacity = max(2, 5 * row_count // (4 * owners))
    rows_x = slowness.shape[0]
    rows_y = slowness.shape[1]
    cell_count = rows_x * rows_y
    row_ids = jnp.arange(row_count, dtype=jnp.int32)
    same_owner = (trace_owner[:, None] == trace_owner[None, :]) & (
        row_ids[None, :] < row_ids[:, None]
    )
    owner_rank = jnp.sum(same_owner.astype(jnp.int32), axis=1)
    slot_index = trace_owner * capacity + owner_rank
    send_traces = jnp.zeros((owners * capacity, samples), jnp.bfloat16).at[slot_index].set(traces)
    send_offsets = jnp.zeros((owners * capacity,), jnp.bfloat16).at[slot_index].set(trace_offset)
    send_cells = (
        jnp.zeros((owners * capacity,), jnp.bfloat16)
        .at[slot_index]
        .set((trace_cell + 1).astype(jnp.bfloat16))
    )
    slow_table = slowness.reshape(cell_count, samples)
    cell_ids = jnp.arange(cell_count, dtype=jnp.int32)
    shaped = (
        send_traces.reshape(owners, capacity, samples),
        send_offsets.reshape(owners, capacity),
        send_cells.reshape(owners, capacity),
    )
    got_traces = lax.all_to_all(
        shaped[0], ("xline", "iline"), split_axis=0, concat_axis=0, tiled=True
    )
    got_offsets = lax.all_to_all(
        shaped[1], ("xline", "iline"), split_axis=0, concat_axis=0, tiled=True
    )
    got_cells = lax.all_to_all(
        shaped[2], ("xline", "iline"), split_axis=0, concat_axis=0, tiled=True
    )
    sources = got_offsets.shape[0]
    item_count = got_offsets.shape[1]
    flat_cells = got_cells.reshape(sources * item_count).astype(jnp.int32) - 1
    picker = (flat_cells[:, None] == cell_ids[None, :]).astype(jnp.float32)
    slow_rows = jnp.dot(picker, slow_table, precision=lax.Precision.HIGHEST)
    moved = corrected_rows(
        got_traces.reshape(sources * item_count, samples),
        got_offsets.reshape(sources * item_count).astype(jnp.float32),
        slow_rows,
        band_start,
    )
    moved_out = moved.reshape(sources, item_count, samples)
    stacked_cells = got_cells.reshape(owners * capacity).astype(jnp.int32) - 1
    members = (cell_ids[:, None] == stacked_cells[None, :]).astype(jnp.float32)
    bin_sums = jnp.dot(
        members, moved_out.reshape(owners * capacity, samples), precision=lax.Precision.HIGHEST
    )
    fold_count = jnp.sum(members, axis=1)
    bin_stack = (bin_sums / jnp.maximum(fold_count, 1.0)[:, None]).reshape(rows_x, rows_y, samples)
    padded = with_halo(bin_stack, (("xline", 0), ("iline", 1)), 1)
    return smooth_bins(padded, dip_shift, rows_x, rows_y)


def solution(mesh):
    return jax.shard_map(
        body,
        mesh=mesh,
        in_specs=(
            P(("xline", "iline"), None),
            P(("xline", "iline")),
            P(("xline", "iline")),
            P(("xline", "iline")),
            P("xline", "iline", None),
            P(),
            P(None, "xline", "iline"),
        ),
        out_specs=P("xline", "iline", None),
        check_vma=False,
    )
```

profile of v0, /device:TPU:0, one launch (start us, length us, event | category | flops | bytes accessed | tf_op | source)
XLA Modules:
  0.0 147.5 jit_solution(3991508899731452529)
XLA Ops:
  0.0 1.0 convert_reduce_fusion
  1.0 0.7 compare_select_fusion
  1.7 3.8 %scatter_custom_fusion = bf16[640]{0:T(1024)(128)(2,1)S(1)} fusion(s32[512]{0:T(512)S(1)} %get-tuple-element.160, bf16[512]{0:T(512)(128)(2,1)S(1)} %get-tuple-element.161, bf16[]{:T(256)} %constant.36.clone.1), kind=kCustom, calls=%fused_computation.272 | custom fusion | bytes 1282 | tf_op jit(solution)/shard_map/scatter | solution.py:88
  5.5 0.7 all_to_all.20
  6.2 7.3 %all-to-all-start = ((bf16[32,1,20]{2,1,0:T(2,128)(2,1)}), bf16[32,1,20]{2,1,0:T(2,128)(2,1)S(1)}, u32[]{:S(2)}, u32[]{:S(2)}) async-start(bf16[32,1,20]{2,1,0:T(2,128)(2,1)} %all_to_all.20), calls=%async_computation | async-start | bytes 32768 | tf_op jit(solution)/shard_map/all_to_all | solution.py:103
  13.5 3.9 %scatter_custom_fusion.1 = bf16[640]{0:T(1024)(128)(2,1)S(1)} fusion(s32[512]{0:T(512)S(1)} %get-tuple-element.160, bf16[512]{0:T(512)(128)(2,1)} %param.8, bf16[]{:T(256)} %constant.36.clone.1), kind=kCustom, calls=%fused_computation.270 | custom fusion | bytes 1792 | tf_op jit(solution)/shard_map/scatter | solution.py:84
  17.4 0.7 all_to_all.21
  18.2 2.4 %all-to-all-done = bf16[32,1,20]{2,1,0:T(2,128)(2,1)S(1)} async-done(((bf16[32,1,20]{2,1,0:T(2,128)(2,1)}), bf16[32,1,20]{2,1,0:T(2,128)(2,1)S(1)}, u32[]{:S(2)}, u32[]{:S(2)}) %all-to-all-start) | async-done | bytes 1312 | tf_op jit(solution)/shard_map/all_to_all | solution.py:103
  20.6 3.4 %all-to-all-start.1 = ((bf16[32,1,20]{2,1,0:T(2,128)(2,1)}), bf16[32,1,20]{2,1,0:T(2,128)(2,1)S(1)}, u32[]{:S(2)}, u32[]{:S(2)}) async-start(bf16[32,1,20]{2,1,0:T(2,128)(2,1)} %all_to_all.21), calls=%async_computation.1 | async-start | bytes 32768 | tf_op jit(solution)/shard_map/all_to_all | solution.py:100
  24.0 4.4 %scatter_custom_fusion.2 = bf16[640,1536]{1,0:T(8,128)(2,1)S(1)} fusion(s32[512]{0:T(512)S(1)} %get-tuple-element.160, bf16[512,1536]{1,0:T(8,128)(2,1)} %param.7, bf16[]{:T(256)} %constant.36.clone.1), kind=kCustom, calls=%fused_computation.58 | custom fusion | bytes 1966592 | tf_op jit(solution)/shard_map/scatter | solution.py:83
  28.4 0.0 copy-start.1
  28.5 0.0 copy-start.2
  28.5 2.1 %reshape.689 = bf16[32,20,1536]{2,1,0:T(8,128)(2,1)} reshape(bf16[640,1536]{1,0:T(8,128)(2,1)S(1)} %scatter_custom_fusion.2) | data formatting | bytes 3932160 | tf_op jit(solution)/shard_map/reshape | solution.py:93
  30.6 0.6 all-to-all-done.1
  31.2 5.4 %all-to-all-start.2 = ((bf16[32,20,1536]{2,1,0:T(8,128)(2,1)}), bf16[32,20,1536]{2,1,0:T(8,128)(2,1)S(1)}, u32[]{:S(2)}, u32[]{:S(2)}) async-start(bf16[32,20,1536]{2,1,0:T(8,128)(2,1)} %reshape.689), calls=%async_computation.2 | async-start | bytes 4718592 | tf_op jit(solution)/shard_map/all_to_all | solution.py:97
  36.6 0.0 copy-done.1
  36.7 0.0 copy-done.2
  36.8 0.1 add_reduce_fusion
  36.9 0.1 sub.130
  37.0 0.1 multiply_reduce_fusion
  37.0 0.1 mul.150
  37.1 0.1 convert_reduce_fusion.1
  37.2 3.6 %fusion.48 = f32[640,1536]{1,0:T(8,128)} fusion(f32[8,1536]{1,0:T(8,128)S(1)} %reshape.688, s32[640]{0:T(1024)S(1)} %sub.130), kind=kOutput, calls=%fused_computation.61 | convolution fusion | flops 94376960 | bytes 3983872 | tf_op jit(solution)/shard_map/dot_general | solution.py:110
  40.9 50.0 %all-to-all-done.2 = bf16[32,20,1536]{2,1,0:T(8,128)(2,1)S(1)} async-done(((bf16[32,20,1536]{2,1,0:T(8,128)(2,1)}), bf16[32,20,1536]{2,1,0:T(8,128)(2,1)S(1)}, u32[]{:S(2)}, u32[]{:S(2)}) %all-to-all-start.2) | async-done | bytes 1966112 | tf_op jit(solution)/shard_map/all_to_all | solution.py:97
  90.9 2.0 %reshape.690 = bf16[640,1536]{1,0:T(8,128)(2,1)} reshape(bf16[32,20,1536]{2,1,0:T(8,128)(2,1)S(1)} %all-to-all-done.2) | data formatting | bytes 3932160 | tf_op jit(solution)/shard_map/reshape | solution.py:112
  92.9 0.0 copy-start
  92.9 34.1 %fusion.1 = f32[8,1536]{1,0:T(8,128)S(1)} fusion(bf16[640,1536]{1,0:T(8,128)(2,1)} %reshape.690, f32[640,1536]{1,0:T(8,128)} %fusion.48, f32[1536]{0:T(1024)S(1)} %get-tuple-element.162, f32[1536]{0:T(1024)S(1)} %get-tuple-element.163, f32[1536]{0:T(1024)S(1)} %get-tuple-element.164, f32[1536]{0:T(1024)S(1)} %get-tuple-element.165, ...), kind=kOutput, calls=%fused_computation.5 | convolution fusion | flops 228082688 | bytes 6073888 | tf_op jit(solution)/shard_map/dot_general | solution.py:120
  127.0 3.2 %collective-permute-start = (f32[1,4,1536]{2,1,0:T(4,128)S(1)}, f32[1,4,1536]{2,1,0:T(4,128)S(1)}, u32[]{:S(2)}, u32[]{:S(2)}) collective-permute-start(f32[1,4,1536]{2,1,0:T(4,128)S(1)} %get-tuple-element.101), channel_id=1, source_target_pairs={{0,4},{4,8},{8,12},{12,16},{16,20},{20,24},{24,28},{1,5},{5,9},{9,... | collective-permute-start | bytes 73736 | tf_op jit(solution)/shard_map/ppermute | solution.py:21
  130.2 0.0 copy-done
  130.2 2.3 %compare_reduce_fusion.80 = (pred[2,4]{1,0:T(4,128)(4,1)S(1)}, pred[2,4]{1,0:T(4,128)(4,1)S(1)}, pred[2,4]{1,0:T(4,128)(4,1)S(1)}, pred[2,4]{1,0:T(4,128)(4,1)S(...) fusion(s32[9,2,4]{0,2,1:T(4,128)S(1)} %copy-done), kind=kLoop, calls=%fused_computation.268 | loop fusion | flops 496 | bytes 784 | tf_op jit(solution)/shard_map/eq | solution.py:60
  132.6 1.3 collective-permute-start.1
  133.9 0.0 collective-permute-done
  133.9 4.4 %collective-permute-done.1 = f32[1,4,1536]{2,1,0:T(4,128)S(1)} collective-permute-done((f32[1,4,1536]{2,1,0:T(4,128)S(1)}, f32[1,4,1536]{2,1,0:T(4,128)S(1)}, u32[]{:S(2)}, u32[]{:S(2)}) %collective-permute-start.1) | collective-permute-done | bytes 24608 | tf_op jit(solution)/shard_map/ppermute | solution.py:22
  138.4 1.3 collective-permute-start.2
  139.7 1.3 collective-permute-start.3
  141.0 0.8 compare_reduce_fusion.53
  141.8 0.0 collective-permute-done.2
  141.8 2.7 %collective-permute-done.3 = f32[4,1,1536]{2,1,0:T(1,128)S(1)} collective-permute-done((f32[4,1,1536]{2,1,0:T(1,128)S(1)}, f32[4,1,1536]{2,1,0:T(1,128)S(1)}, u32[]{:S(2)}, u32[]{:S(2)}) %collective-permute-start.3) | collective-permute-done | bytes 24608 | tf_op jit(solution)/shard_map/ppermute | solution.py:22
  144.5 0.1 pad_maximum_fusion.7
  144.6 2.9 %multiply_add_fusion = f32[2,4,1536]{2,1,0:T(4,128)} fusion(f32[2,4,1536]{2,1,0:T(4,128)S(1)} %get-tuple-element.92, f32[2,4,1536]{2,1,0:T(4,128)S(1)} %get-tuple-element.98, f32[2,4,1536]{2,1,0:T(4,128)S(1)} %get-tuple-element.88, f32[2,4,1536]{2,1,0:T(4,128)S(1)} %get-tuple-element.93, f32[2,4,1536]{2,1,0:T(4,128)S(1)} %reshape.691, ...), kind=kLoop, calls=%fused_computation.71 | loop fusion | flops 2052096 | bytes 492168 | tf_op jit(solution)/shard_map/add | solution.py:65
  (18 shorter events, 0.2 us)
Async XLA Ops:
  6.2 14.4 %all-to-all-start = ((bf16[32,1,20]{2,1,0:T(2,128)(2,1)}), bf16[32,1,20]{2,1,0:T(2,128)(2,1)S(1)}, u32[]{:S(2)}, u32[]{:S(2)}) async-start(bf16[32,1,20]{2,1,0:T(2,128)(2,1)} %all_to_all.20), calls=%async_computation | async-start | bytes 32768 | tf_op jit(solution)/shard_map/all_to_all | solution.py:103
  20.6 10.6 %all-to-all-start.1 = ((bf16[32,1,20]{2,1,0:T(2,128)(2,1)}), bf16[32,1,20]{2,1,0:T(2,128)(2,1)S(1)}, u32[]{:S(2)}, u32[]{:S(2)}) async-start(bf16[32,1,20]{2,1,0:T(2,128)(2,1)} %all_to_all.21), calls=%async_computation.1 | async-start | bytes 32768 | tf_op jit(solution)/shard_map/all_to_all | solution.py:100
  28.4 8.1 %copy-start.1 = (f32[2,4,1536]{2,1,0:T(4,128)S(1)}, f32[2,4,1536]{2,1,0:T(4,128)}, u32[]{:S(2)}) copy-start(f32[2,4,1536]{2,1,0:T(4,128)} %param.11) | copy-start | bytes 147460
  28.5 8.3 %copy-start.2 = (s32[1536]{0:T(1024)S(1)}, s32[1536]{0:T(1024)}, u32[]{:S(2)}) copy-start(s32[1536]{0:T(1024)} %param.12) | copy-start | bytes 18436
  31.2 59.7 %all-to-all-start.2 = ((bf16[32,20,1536]{2,1,0:T(8,128)(2,1)}), bf16[32,20,1536]{2,1,0:T(8,128)(2,1)S(1)}, u32[]{:S(2)}, u32[]{:S(2)}) async-start(bf16[32,20,1536]{2,1,0:T(8,128)(2,1)} %reshape.689), calls=%async_computation.2 | async-start | bytes 4718592 | tf_op jit(solution)/shard_map/all_to_all | solution.py:97
  92.9 37.3 %copy-start = (s32[9,2,4]{0,2,1:T(4,128)S(1)}, s32[9,2,4]{0,2,1:T(4,128)}, u32[]{:S(2)}) copy-start(s32[9,2,4]{0,2,1:T(4,128)} %param.13) | copy-start | bytes 868
  127.0 6.9 %collective-permute-start = (f32[1,4,1536]{2,1,0:T(4,128)S(1)}, f32[1,4,1536]{2,1,0:T(4,128)S(1)}, u32[]{:S(2)}, u32[]{:S(2)}) collective-permute-start(f32[1,4,1536]{2,1,0:T(4,128)S(1)} %get-tuple-element.101), channel_id=1, source_target_pairs={{0,4},{4,8},{8,12},{12,16},{16,20},{20,24},{24,28},{1,5},{5,9},{9,... | collective-permute-start | bytes 73736 | tf_op jit(solution)/shard_map/ppermute | solution.py:21
  132.6 5.7 %collective-permute-start.1 = (f32[1,4,1536]{2,1,0:T(4,128)S(1)}, f32[1,4,1536]{2,1,0:T(4,128)S(1)}, u32[]{:S(2)}, u32[]{:S(2)}) collective-permute-start(f32[1,4,1536]{2,1,0:T(4,128)S(1)} %get-tuple-element.100), channel_id=1, source_target_pairs={{4,0},{8,4},{12,8},{16,12},{20,16},{24,20},{28,24},{5,1},{9,5},{13... | collective-permute-start | bytes 73736 | tf_op jit(solution)/shard_map/ppermute | solution.py:22
  138.4 3.4 %collective-permute-start.2 = (f32[4,1,1536]{2,1,0:T(1,128)S(1)}, f32[4,1,1536]{2,1,0:T(1,128)S(1)}, u32[]{:S(2)}, u32[]{:S(2)}) collective-permute-start(f32[4,1,1536]{2,1,0:T(1,128)S(1)} %get-tuple-element.95), channel_id=1, source_target_pairs={{0,1},{1,2},{2,3},{4,5},{5,6},{6,7},{8,9},{9,10},{10,11},{12,13},{... | collective-permute-start | bytes 73736 | tf_op jit(solution)/shard_map/ppermute | solution.py:21
  139.7 4.8 %collective-permute-start.3 = (f32[4,1,1536]{2,1,0:T(1,128)S(1)}, f32[4,1,1536]{2,1,0:T(1,128)S(1)}, u32[]{:S(2)}, u32[]{:S(2)}) collective-permute-start(f32[4,1,1536]{2,1,0:T(1,128)S(1)} %get-tuple-element.96), channel_id=1, source_target_pairs={{1,0},{2,1},{3,2},{5,4},{6,5},{7,6},{9,8},{10,9},{11,10},{13,12},{... | collective-permute-start | bytes 73736 | tf_op jit(solution)/shard_map/ppermute | solution.py:22
where the time goes:
time: 150 us; the launch traced here: 148 us
  waiting for transfers between devices  60.1 us (40%)
  matrix products  37.7 us (25%)
  starting transfers between devices  23.2 us (15%)
  local copies, waits for them, and re-layouts  17.9 us (12%)
  other arithmetic  8.28 us (6%)
    all_to_all x1, waiting for transfers between devices, body(): lax.all_to_all(shaped[0], ('xline', 'iline'), split_axis=0, concat_axis=0...  50 us
    dot_general x1, matrix products, body(): jnp.dot(members, moved_out.reshape(owners * capacity, samples), precision...  34.1 us
    all_to_all x1, starting transfers between devices, body(): lax.all_to_all(shaped[2], ('xline', 'iline'), split_axis=0, concat_axis=0...  7.3 us
    ppermute x2, waiting for transfers between devices, with_halo(): after = lax.ppermute(initial, axis, down)  7.07 us
    all_to_all x1, starting transfers between devices, body(): lax.all_to_all(shaped[0], ('xline', 'iline'), split_axis=0, concat_axis=0...  5.43 us
    ppermute x2, starting transfers between devices, with_halo(): before = lax.ppermute(last, axis, up)  4.5 us
    scatter x1, local copies, waits for them, and re-layouts, body(): jnp.zeros((owners * capacity, samples), jnp.bfloat16).at[slot_index]  4.43 us
    scatter x1, local copies, waits for them, and re-layouts, body(): jnp.zeros((owners * capacity,), jnp.bfloat16).at[slot_index]  3.92 us
  transfers between devices with their start and end apart: 7, of which 5 were waited for; matrix products, arithmetic and copies ran while one was open for 12% of the time, Pallas kernels for 0%

commit v1 on v0

v1 whole, which is shorter than its diff:
```python
import functools

import jax
import jax.numpy as jnp
from jax import lax
from jax.experimental import pallas as pl
from jax.experimental.pallas import tpu as pltpu
from jax.sharding import PartitionSpec as P

BAND = 8
DIP = 4
HALF = BAND // 2
LANES = 128
CENTER_WEIGHT = 0.5
SIDE_WEIGHT = 0.0625
MESH = pl.DeviceIdType.MESH
NT_DIMS = (((1,), (1,)), ((), ()))
f32 = jnp.float32
bf16 = jnp.bfloat16


def up_to(value, multiple):
    return -(-value // multiple) * multiple


def iota(shape, dim):
    return lax.broadcasted_iota(jnp.int32, shape, dim)


def dot(a, b):
    return jnp.dot(a, b, preferred_element_type=f32)


def parts(value, count):
    out = []
    for _ in range(count):
        piece = value.astype(bf16)
        out.append(piece)
        value = value - piece.astype(f32)
    return out


def kernel(
    c, meta_ref, traces_ref, slow_ref, band_ref, dip_ref, out_ref,
    send, send_meta, recv, recv_meta, slows, slow_parts, gather, picks, slow_rows, moved,
    sums, sums_in, stack, halo, lagged,
    s_send, s_recv, m_send, m_recv, w_send, w_recv, z_send, z_recv, h_send, h_recv,
):
    nx, nil, nz, group, cap, rows, samples = c.nx, c.nil, c.nz, c.group, c.cap, c.rows, c.samples
    ny = nil // 2
    blocks = samples // LANES
    cells = slow_ref.shape[0]
    xl = lax.axis_index("xline")
    il = lax.axis_index("iline")
    z, x = xl // nx, xl % nx
    y, core = il // 2, il % 2

    def plane(k):
        kx, ky, kc = k // nil, (k % nil) // 2, k % 2
        tx = (x + kx) % nx
        ti = ((y + ky) % ny) * 2 + (core + kc) % 2
        return tx, ti

    def plane_id(k):
        tx, ti = plane(k)
        return {"xline": z * nx + tx, "iline": ti}

    def z_id(k):
        return {"xline": ((z + k) % nz) * nx + x, "iline": il}

    around = [(dx, dy) for dx in (-1, 0, 1) for dy in (-1, 0, 1) if (dx, dy) != (0, 0)]

    def valid(dx, dy):
        ok = None
        for at, step, size in ((xl, dx, nx * nz), (il, dy, nil)):
            if step:
                here = (at + step >= 0) & (at + step < size)
                ok = here if ok is None else ok & here
        return ok

    def near_id(dx, dy):
        return {"xline": xl + dx, "iline": il + dy}

    barrier = pltpu.get_barrier_semaphore()

    def greet(target):
        pl.semaphore_signal(barrier, inc=1, device_id=target, device_id_type=MESH)

    lax.fori_loop(1, group, lambda k, _: (greet(plane_id(k)), 0)[1], 0)
    lax.fori_loop(1, nz, lambda k, _: (greet(z_id(k)), 0)[1], 0)
    for dx, dy in around:
        pl.when(valid(dx, dy))(functools.partial(lambda t: greet(t), near_id(dx, dy)))

    meta = meta_ref[...]
    owner_row, base_row = meta[0:1, :], meta[1:2, :]
    count = meta.shape[1]
    owners = up_to(group * nz, 16)
    mine = jnp.where(iota((owners, count), 0).astype(f32) == owner_row, 1.0, 0.0)
    earlier = jnp.where(iota((count, count), 0) < iota((count, count), 1), 1.0, 0.0).astype(bf16)
    before = dot(mine.astype(bf16), earlier)
    slot = base_row + jnp.sum(mine * before, axis=0, keepdims=True)
    values = jnp.concatenate([meta[2:4, :], jnp.zeros((14, count), f32)], axis=0).astype(bf16)

    def span_of(at, size):
        return 3 - jnp.where(at == 0, 1, 0) - jnp.where(at == size - 1, 1, 0)

    near = span_of(xl, nx * nz) * span_of(il, nil) - 1
    pl.semaphore_wait(barrier, (group - 1) + (nz - 1) + near)

    def slow_copy(k):
        return pltpu.make_async_remote_copy(
            src_ref=slow_ref, dst_ref=slows.at[z], send_sem=w_send.at[k], recv_sem=w_recv.at[k],
            device_id=z_id(k), device_id_type=MESH,
        )

    def row_copy(k):
        return pltpu.make_async_remote_copy(
            src_ref=send.at[k], dst_ref=recv.at[pl.ds(pl.multiple_of(k * rows, 16), rows), pl.ds(0, samples)],
            send_sem=s_send.at[k], recv_sem=s_recv.at[k], device_id=plane_id(k), device_id_type=MESH,
        )

    def meta_copy(k):
        return pltpu.make_async_remote_copy(
            src_ref=send_meta.at[k], dst_ref=recv_meta.at[k],
            send_sem=m_send.at[k], recv_sem=m_recv.at[k], device_id=plane_id(k), device_id_type=MESH,
        )

    lax.fori_loop(1, nz, lambda k, _: (slow_copy(k).start(), 0)[1], 0)

    def pack(k):
        tx, ti = plane(k)
        first = ((tx * nil + ti) * rows).astype(f32)
        hot = jnp.where(iota((c.meta_rows, count), 0).astype(f32) + first == slot, 1.0, 0.0).astype(bf16)
        chunk = dot(hot[:rows], traces_ref[...])
        chunk = pltpu.roll(chunk, LANES // 2, 1).astype(bf16)
        info = lax.dot_general(values, hot, NT_DIMS, preferred_element_type=f32).astype(bf16)
        return chunk, info

    def send_one(k, _):
        chunk, info = pack(k)
        send[k] = chunk
        send_meta[k] = info
        meta_copy(k).start()
        row_copy(k).start()
        return 0

    lax.fori_loop(1, group, send_one, 0)
    chunk, info = pack(0)
    recv[0:rows, 0:samples] = chunk
    recv_meta[0] = info

    def make_gather(b, _):
        start = pl.multiple_of(b * LANES, LANES)
        position = band_ref[:, pl.ds(start, LANES)] - start + LANES // 2
        window = iota((2 * LANES, LANES), 0)
        for pair in range(HALF):
            first = jnp.where(window == position + pair, 1.0, 0.0)
            last = jnp.where(window == position + (BAND - 1 - pair), 1.0, 0.0)
            at = pair * 2 * LANES
            gather[b, :, at : at + LANES] = (first + last).astype(bf16)
            gather[b, :, at + LANES : at + 2 * LANES] = ((first - last) * float(BAND - 1 - 2 * pair)).astype(bf16)
        return 0

    lax.fori_loop(0, blocks, make_gather, 0)

    slows[pl.ds(z, 1)] = slow_ref[...][None]
    lax.fori_loop(1, nz, lambda k, _: (slow_copy(k).wait_recv(), 0)[1], 0)
    bins = nz * cells
    table = slows[...].reshape(bins, samples)
    for i, piece in enumerate(parts(table, 3)):
        slow_parts[i * bins : (i + 1) * bins, :] = piece
    slow_parts[3 * bins :, :] = jnp.zeros((bins, samples), bf16)

    sums[...] = jnp.zeros_like(sums)
    batch = c.batch
    batch_rows = batch * rows
    tile = 32 if batch_rows % 32 == 0 else 16

    def one_batch(i, _):
        for j in range(batch):
            k = i * batch + j

            @pl.when(k > 0)
            def _():
                meta_copy(k).wait_recv()
                row_copy(k).wait_recv()

        span = pl.ds(pl.multiple_of(i * batch_rows, 16), batch_rows)
        recv[span, samples : samples + LANES] = recv[span, 0:LANES]
        same = jnp.where(iota((rows, c.meta_rows), 0) == iota((rows, c.meta_rows), 1), 1.0, 0.0).astype(bf16)
        columns = jnp.concatenate(
            [
                lax.dot_general(same, recv_meta[i * batch + j], NT_DIMS, preferred_element_type=f32)
                for j in range(batch)
            ],
            axis=0,
        )
        offset = columns[:, 0:1]
        cell = columns[:, 1:2]
        step = iota((batch_rows, 1), 0)
        base = jnp.zeros((batch_rows, 1), f32)
        for j in range(batch):
            for owner in range(1, nz):
                base = base + jnp.where((step >= j * rows + owner * cap) & (step < (j + 1) * rows), float(cells), 0.0)
        bin_id = jnp.where(cell > 0.5, base + cell - 1.0, -1.0)
        lane = iota((1, 4 * bins), 1)
        members = jnp.where((lane % bins).astype(f32) == bin_id, 1.0, 0.0).astype(bf16)
        eye = jnp.where(iota((bins, 4 * bins), 0) == iota((bins, 4 * bins), 1), 1.0, 0.0).astype(bf16)
        turned = lax.dot_general(eye, members, NT_DIMS, preferred_element_type=f32)
        fold = jnp.sum(turned, axis=1, keepdims=True)
        turned = turned.astype(bf16)
        last = pl.ds(samples, LANES)
        sums[:, :, last] = sums[:, :, last] + jnp.broadcast_to(fold, (bins, LANES)).reshape(nz, cells, LANES)
        offset2 = jnp.broadcast_to(offset * offset, (batch_rows, LANES))
        moved[2] = offset2

        def one_block(b, _):
            start = pl.multiple_of(b * LANES, LANES)
            lanes = pl.ds(start, LANES)
            picks[...] = dot(recv[span, pl.ds(start, 2 * LANES)], gather[b])
            slow_rows[...] = dot(members, slow_parts[:, lanes])
            time = (iota((1, LANES), 1) + start).astype(f32)
            time2 = time * time
            center = band_ref[:, lanes].astype(f32) + 0.5 * (BAND - 1)

            def one_tile(r, _):
                here = pl.ds(pl.multiple_of(r * tile, 16), tile)
                moveout = jnp.sqrt(time2 + moved[2, here, :] * slow_rows[here, :])
                off = center - moveout
                u = off * off
                u2 = u * u
                terms = []
                for pair in range(HALF):
                    reach = 0.5 * (BAND - 1) - pair
                    at = pair * 2 * LANES
                    v = u + (1.0 + reach * reach)
                    n = v * picks[here, at : at + LANES] + off * picks[here, at + LANES : at + 2 * LANES]
                    q = u2 + ((2.0 - 2.0 * reach * reach) * u + (1.0 + reach * reach) ** 2)
                    terms.append((n, v, q))
                while len(terms) > 1:
                    merged = []
                    for (n1, v1, q1), (n2, v2, q2) in zip(terms[::2], terms[1::2]):
                        q = None if len(terms) == 2 else q1 * q2
                        merged.append((n1 * q2 + n2 * q1, v1 * q2 + v2 * q1, q))
                    terms = merged
                n, v, _q = terms[0]
                moved[0, here, :] = n / (v + v)
                return 0

            lax.fori_loop(0, batch_rows // tile, one_tile, 0, unroll=True)
            high, low = parts(moved[0], 2)
            total = dot(turned, high) + dot(turned, low)
            sums[:, :, lanes] = sums[:, :, lanes] + total.reshape(nz, cells, LANES)
            return 0

        lax.fori_loop(0, blocks, one_block, 0)
        return 0

    lax.fori_loop(0, group // batch, one_batch, 0)

    def sum_copy(k):
        return pltpu.make_async_remote_copy(
            src_ref=sums.at[(z + k) % nz], dst_ref=sums_in.at[k - 1],
            send_sem=z_send.at[k], recv_sem=z_recv.at[k], device_id=z_id(k), device_id_type=MESH,
        )

    lax.fori_loop(1, nz, lambda k, _: (sum_copy(k).start(), 0)[1], 0)
    total = sums[pl.ds(z, 1)][0]
    for k in range(1, nz):
        sum_copy(k).wait_recv()
        total = total + sums_in[k - 1]
    stack[...] = total[:, :samples] / jnp.maximum(total[:, samples : samples + 1], 1.0)

    def halo_copy(i, dx, dy):
        return pltpu.make_async_remote_copy(
            src_ref=stack, dst_ref=halo.at[len(around) - 1 - i],
            send_sem=h_send.at[i], recv_sem=h_recv.at[len(around) - 1 - i],
            device_id=near_id(dx, dy), device_id_type=MESH,
        )

    def halo_wait(i):
        return pltpu.make_async_remote_copy(
            src_ref=stack, dst_ref=halo.at[i], send_sem=h_send.at[i], recv_sem=h_recv.at[i],
            device_id=near_id(*around[i]), device_id_type=MESH,
        )

    for i, (dx, dy) in enumerate(around):
        pl.when(valid(dx, dy))(functools.partial(lambda i, dx, dy: halo_copy(i, dx, dy).start(), i, dx, dy))

    bx, by = c.bx, c.by
    wide = by + 2
    padded_rows = (bx + 2) * wide
    lag_rows = up_to(padded_rows, 8)
    lags = 2 * DIP + 1
    lane = iota((cells, lagged.shape[0]), 1)
    place = iota((cells, 1), 0)
    weights = jnp.zeros(lane.shape, f32)
    for n in range(9):
        spot = jnp.zeros((cells, 1), jnp.int32)
        for b in range(cells):
            p = (b // by + n // 3) * wide + b % by + n % 3
            spot = jnp.where(place == b, p, spot)
        spot = spot + (dip_ref[:, n : n + 1] + DIP) * lag_rows
        weights = weights + jnp.where(lane == spot, CENTER_WEIGHT if n == 4 else SIDE_WEIGHT, 0.0)
    weights = weights.astype(bf16)
    if lagged.shape[0] > lags * lag_rows:
        lagged[lags * lag_rows :, :] = jnp.zeros((lagged.shape[0] - lags * lag_rows, samples), f32)

    for i, (dx, dy) in enumerate(around):
        ok = valid(dx, dy)
        pl.when(ok)(functools.partial(lambda i: halo_wait(i).wait_recv(), i))

        @pl.when(jnp.logical_not(ok))
        def _():
            halo[i] = jnp.zeros((cells, samples), f32)

    lines = []
    for px in range(bx + 2):
        for py in range(wide):
            dx = -1 if px == 0 else (1 if px == bx + 1 else 0)
            dy = -1 if py == 0 else (1 if py == wide - 1 else 0)
            line = (px - 1 - dx * bx) * by + (py - 1 - dy * by)
            block = stack if (dx, dy) == (0, 0) else halo.at[around.index((dx, dy))]
            lines.append(block[line : line + 1, :])
    lines += [jnp.zeros((1, samples), f32)] * (lag_rows - padded_rows)
    padded = jnp.concatenate(lines, axis=0)
    time = iota((lag_rows, samples), 1)
    for i in range(lags):
        lag = i - DIP
        shifted = padded if lag == 0 else pltpu.roll(padded, (-lag) % samples, 1)
        inside = (time + lag >= 0) & (time + lag < samples)
        lagged[i * lag_rows : (i + 1) * lag_rows, :] = jnp.where(inside, shifted, 0.0)
    result = sum(dot(weights, piece) for piece in parts(lagged[...], 3))
    for row in range(bx):
        out_ref[row] = result[row * by : (row + 1) * by, :]

    def done_plane(k, _):
        meta_copy(k).wait_send()
        row_copy(k).wait_send()
        return 0

    def done_z(k, _):
        slow_copy(k).wait_send()
        sum_copy(k).wait_send()
        return 0

    lax.fori_loop(1, group, done_plane, 0)
    lax.fori_loop(1, nz, done_z, 0)
    for i, (dx, dy) in enumerate(around):
        pl.when(valid(dx, dy))(functools.partial(lambda i, dx, dy: halo_copy(i, dx, dy).wait_send(), i, dx, dy))


class Sizes:
    pass


def body(sizes, traces, trace_offset, trace_owner, trace_cell, slowness, band_start, dip_shift):
    c = Sizes()
    size_x, c.nil = sizes
    c.nz = 1
    while c.nz * c.nz < size_x:
        c.nz *= 2
    c.nx = size_x // c.nz
    c.group = c.nx * c.nil
    count, c.samples = traces.shape
    c.cap = max(2, 5 * count // (4 * size_x * c.nil))
    c.rows = up_to(c.nz * c.cap, 16)
    c.meta_rows = up_to(c.rows, LANES)
    c.bx, c.by = slowness.shape[:2]
    c.batch = 2
    cells = c.bx * c.by
    bins = c.nz * cells
    base = (trace_owner % c.group) * c.rows + (trace_owner // c.group) * c.cap
    zero = jnp.zeros((count,), f32)
    meta = jnp.stack(
        [trace_owner.astype(f32), base.astype(f32), trace_offset.astype(f32), (trace_cell + 1).astype(f32)]
        + [zero] * 4
    )
    dips = dip_shift.reshape(9, cells).T
    samples = c.samples
    blocks = samples // LANES
    batch_rows = c.batch * c.rows
    lag_rows = up_to((c.bx + 2) * (c.by + 2), 8)
    dma = pltpu.SemaphoreType.DMA
    return pl.pallas_call(
        functools.partial(kernel, c),
        out_shape=jax.ShapeDtypeStruct((c.bx, c.by, samples), f32),
        in_specs=[pl.BlockSpec(memory_space=pltpu.VMEM)] * 5,
        out_specs=pl.BlockSpec(memory_space=pltpu.VMEM),
        scratch_shapes=[
            pltpu.VMEM((c.group, c.rows, samples), bf16),
            pltpu.VMEM((c.group, 16, c.meta_rows), bf16),
            pltpu.VMEM((c.group * c.rows, samples + LANES), bf16),
            pltpu.VMEM((c.group, 16, c.meta_rows), bf16),
            pltpu.VMEM((c.nz, cells, samples), f32),
            pltpu.VMEM((4 * bins, samples), bf16),
            pltpu.VMEM((blocks, 2 * LANES, BAND * LANES), bf16),
            pltpu.VMEM((batch_rows, BAND * LANES), f32),
            pltpu.VMEM((batch_rows, LANES), f32),
            pltpu.VMEM((3, batch_rows, LANES), f32),
            pltpu.VMEM((c.nz, cells, samples + LANES), f32),
            pltpu.VMEM((c.nz - 1, cells, samples + LANES), f32),
            pltpu.VMEM((cells, samples), f32),
            pltpu.VMEM((8, cells, samples), f32),
            pltpu.VMEM((up_to((2 * DIP + 1) * lag_rows, LANES), samples), f32),
            dma((c.group,)), dma((c.group,)), dma((c.group,)), dma((c.group,)),
            dma((c.nz,)), dma((c.nz,)), dma((c.nz,)), dma((c.nz,)),
            dma((8,)), dma((8,)),
        ],
        compiler_params=pltpu.CompilerParams(
            collective_id=0, has_side_effects=True, vmem_limit_bytes=48 * 1024 * 1024
        ),
        name="bin_stack_smooth",
    )(meta, traces, slowness.reshape(cells, samples), band_start.reshape(1, samples), dips)


def solution(mesh):
    sizes = (mesh.shape["xline"], mesh.shape["iline"])
    return jax.shard_map(
        functools.partial(body, sizes),
        mesh=mesh,
        in_specs=(
            P(("xline", "iline"), None),
            P(("xline", "iline")),
            P(("xline", "iline")),
            P(("xline", "iline")),
            P("xline", "iline", None),
            P(),
            P(None, "xline", "iline"),
        ),
        out_specs=P("xline", "iline", None),
        check_vma=False,
    )
```

time: 150 us -> 61.3 us (0.41)
  the two profiles are of different devices: /device:TPU:0 before, /device:TPU:12 now
where the time goes in v1:
time: 61.3 us; the launch traced here: 61 us
  Pallas kernels  54.6 us (89%)
  local copies, waits for them, and re-layouts  4.27 us (7%)
  other arithmetic  2.13 us (3%)
    pallas_call x1, Pallas kernels, body(): pl.pallas_call(functools.partial(kernel, c), out_shape=jax.ShapeDtypeStru...  54.6 us
    unnamed x5, local copies, waits for them, and re-layouts  2.71 us

profile of v1, /device:TPU:12, one launch (start us, length us, event | category | flops | bytes accessed | tf_op | source)
XLA Modules:
  0.0 61.0 jit_solution(1681152351983962253)
XLA Ops:
  0.0 0.7 %stack.28 = f32[512]{0:T(512)S(1)} convert(bf16[512]{0:T(512)(128)(2,1)} %param.8) | non-fusion elementwise | flops 512 | bytes 3072 | tf_op jit(solution)/shard_map/stack | solution.py:375
  0.7 0.7 %add_convert_fusion = f32[512]{0:T(512)S(1)} fusion(s32[512]{0:T(512)} %param.10), kind=kLoop, calls=%fused_computation.9 | loop fusion | flops 1024 | bytes 4096 | tf_op jit(solution)/shard_map/convert_element_type | solution.py:376
  1.4 0.8 %fusion.2 = (f32[512]{0:T(512)S(1)}, f32[512]{0:T(512)S(1)}) fusion(s32[512]{0:T(512)} %param.9), kind=kLoop, calls=%fused_computation.7 | loop fusion | flops 12288 | bytes 6144 | tf_op jit(solution)/shard_map/convert_element_type | solution.py:376
  2.1 0.7 %reshape.10.band_ref = s32[1,1536]{1,0:T(1,128)S(1)} reshape(s32[1536]{0:T(1024)} %param.12) | data formatting | bytes 12288 | tf_op jit(solution)/shard_map/reshape | solution.py:414
  2.9 0.8 %reshape.9.slow_ref = f32[8,1536]{1,0:T(8,128)S(1)} reshape(f32[2,4,1536]{2,1,0:T(4,128)} %param.11) | data formatting | bytes 98304 | tf_op jit(solution)/shard_map/reshape | solution.py:414
  3.7 0.0 copy-start
  3.7 1.4 %copy-done = bf16[512,1536]{1,0:T(8,128)(2,1)S(1)} copy-done((bf16[512,1536]{1,0:T(8,128)(2,1)S(1)}, bf16[512,1536]{1,0:T(8,128)(2,1)}, u32[]{:S(2)}) %copy-start) | copy-done | bytes 1572888
  5.1 0.0 copy-start.1
  5.1 0.7 %copy-done.1 = s32[9,2,4]{0,2,1:T(4,128)S(1)} copy-done((s32[9,2,4]{0,2,1:T(4,128)S(1)}, s32[9,2,4]{0,2,1:T(4,128)}, u32[]{:S(2)}) %copy-start.1) | copy-done | bytes 312
  5.8 54.6 %bin_stack_smooth.1 = f32[2,4,1536]{2,1,0:T(4,128)S(1)} custom-call(f32[8,512]{1,0:T(8,128)S(1)} %stack.27.meta_ref, bf16[512,1536]{1,0:T(8,128)(2,1)S(1)} %copy-done, f32[8,1536]{1,0:T(8,128)S(1)} %reshape.9.slow_ref, s32[1,1536]{1,0:T(1,128)S(1)} %reshape.10.band_ref, s32[8,9]{1,0:T(8,128)S(1)} %bitcast.7), custom_call_target="tpu_custom_call" | custom-call | tf_op jit(solution)/shard_map/bin_stack_smooth/pallas_call | solution.py:385
  60.4 0.6 %copy.9 = f32[2,4,1536]{2,1,0:T(4,128)} copy(f32[2,4,1536]{2,1,0:T(4,128)S(1)} %bin_stack_smooth.1) | data formatting | bytes 98304
  (2 shorter events, 0.0 us)
Async XLA Ops:
  3.7 1.4 %copy-start = (bf16[512,1536]{1,0:T(8,128)(2,1)S(1)}, bf16[512,1536]{1,0:T(8,128)(2,1)}, u32[]{:S(2)}) copy-start(bf16[512,1536]{1,0:T(8,128)(2,1)} %traces_ref.1) | copy-start | bytes 4718596
  5.1 0.7 %copy-start.1 = (s32[9,2,4]{0,2,1:T(4,128)S(1)}, s32[9,2,4]{0,2,1:T(4,128)}, u32[]{:S(2)}) copy-start(s32[9,2,4]{0,2,1:T(4,128)} %param.13) | copy-start | bytes 868

commit v2 on v1

--- a/solution.py
+++ b/solution.py
@@ -41,10 +41,10 @@
 
 
 def kernel(
-    c, meta_ref, traces_ref, slow_ref, band_ref, dip_ref, out_ref,
-    send, send_meta, recv, recv_meta, slows, slow_parts, gather, picks, slow_rows, moved,
+    c, owner_ref, offset_ref, cell_ref, traces_hbm, slow_in, band_in, dip_ref, out_ref,
+    traces_ref, slow_ref, band_ref, send, send_meta, recv, recv_meta, slows, slow_parts, gather, picks, slow_rows, moved,
     sums, sums_in, stack, halo, lagged,
-    s_send, s_recv, m_send, m_recv, w_send, w_recv, z_send, z_recv, h_send, h_recv,
+    t_sem, s_send, s_recv, m_send, m_recv, w_send, w_recv, z_send, z_recv, h_send, h_recv,
 ):
     nx, nil, nz, group, cap, rows, samples = c.nx, c.nil, c.nz, c.group, c.cap, c.rows, c.samples
     ny = nil // 2
@@ -81,6 +81,9 @@
     def near_id(dx, dy):
         return {"xline": xl + dx, "iline": il + dy}
 
+    traces_copy = pltpu.make_async_copy(traces_hbm, traces_ref, t_sem)
+    traces_copy.start()
+
     barrier = pltpu.get_barrier_semaphore()
 
     def greet(target):
@@ -91,15 +94,21 @@
     for dx, dy in around:
         pl.when(valid(dx, dy))(functools.partial(lambda t: greet(t), near_id(dx, dy)))
 
-    meta = meta_ref[...]
-    owner_row, base_row = meta[0:1, :], meta[1:2, :]
-    count = meta.shape[1]
+    count = traces_ref.shape[0]
+    for line in range(c.bx):
+        slow_ref[line * c.by : (line + 1) * c.by, :] = slow_in[line]
+    band_ref[...] = band_in[...].reshape(1, samples)
+    owner_row = owner_ref[...].reshape(1, count).astype(f32)
+    turn = jnp.floor((owner_row + 0.5) * (1.0 / group))
+    base_row = (owner_row - turn * group) * rows + turn * cap
+    offset_row = offset_ref[...].astype(f32).reshape(1, count)
+    cell_row = cell_ref[...].reshape(1, count).astype(f32) + 1.0
     owners = up_to(group * nz, 16)
     mine = jnp.where(iota((owners, count), 0).astype(f32) == owner_row, 1.0, 0.0)
     earlier = jnp.where(iota((count, count), 0) < iota((count, count), 1), 1.0, 0.0).astype(bf16)
     before = dot(mine.astype(bf16), earlier)
     slot = base_row + jnp.sum(mine * before, axis=0, keepdims=True)
-    values = jnp.concatenate([meta[2:4, :], jnp.zeros((14, count), f32)], axis=0).astype(bf16)
+    values = jnp.concatenate([offset_row, cell_row, jnp.zeros((14, count), f32)], axis=0).astype(bf16)
 
     def span_of(at, size):
         return 3 - jnp.where(at == 0, 1, 0) - jnp.where(at == size - 1, 1, 0)
@@ -144,6 +153,7 @@
         row_copy(k).start()
         return 0
 
+    traces_copy.wait()
     lax.fori_loop(1, group, send_one, 0)
     chunk, info = pack(0)
     recv[0:rows, 0:samples] = chunk
@@ -214,18 +224,21 @@
         offset2 = jnp.broadcast_to(offset * offset, (batch_rows, LANES))
         moved[2] = offset2
 
-        def one_block(b, _):
+        def fetch(b, at):
+            start = pl.multiple_of(b * LANES, LANES)
+            picks[at] = dot(recv[span, pl.ds(start, 2 * LANES)], gather[b])
+            slow_rows[at] = dot(members, slow_parts[:, pl.ds(start, LANES)])
+
+        def one_block(b, at_slot):
             start = pl.multiple_of(b * LANES, LANES)
             lanes = pl.ds(start, LANES)
-            picks[...] = dot(recv[span, pl.ds(start, 2 * LANES)], gather[b])
-            slow_rows[...] = dot(members, slow_parts[:, lanes])
             time = (iota((1, LANES), 1) + start).astype(f32)
             time2 = time * time
             center = band_ref[:, lanes].astype(f32) + 0.5 * (BAND - 1)
 
             def one_tile(r, _):
                 here = pl.ds(pl.multiple_of(r * tile, 16), tile)
-                moveout = jnp.sqrt(time2 + moved[2, here, :] * slow_rows[here, :])
+                moveout = jnp.sqrt(time2 + moved[2, here, :] * slow_rows[at_slot, here, :])
                 off = center - moveout
                 u = off * off
                 u2 = u * u
@@ -234,7 +247,7 @@
                     reach = 0.5 * (BAND - 1) - pair
                     at = pair * 2 * LANES
                     v = u + (1.0 + reach * reach)
-                    n = v * picks[here, at : at + LANES] + off * picks[here, at + LANES : at + 2 * LANES]
+                    n = v * picks[at_slot, here, at : at + LANES] + off * picks[at_slot, here, at + LANES : at + 2 * LANES]
                     q = u2 + ((2.0 - 2.0 * reach * reach) * u + (1.0 + reach * reach) ** 2)
                     terms.append((n, v, q))
                 while len(terms) > 1:
@@ -244,16 +257,25 @@
                         merged.append((n1 * q2 + n2 * q1, v1 * q2 + v2 * q1, q))
                     terms = merged
                 n, v, _q = terms[0]
-                moved[0, here, :] = n / (v + v)
+                moved[at_slot, here, :] = n / (v + v)
                 return 0
 
             lax.fori_loop(0, batch_rows // tile, one_tile, 0, unroll=True)
-            high, low = parts(moved[0], 2)
+            high, low = parts(moved[at_slot], 2)
             total = dot(turned, high) + dot(turned, low)
             sums[:, :, lanes] = sums[:, :, lanes] + total.reshape(nz, cells, LANES)
+
+        fetch(0, 0)
+
+        def two_blocks(i, _):
+            b = 2 * i
+            fetch(b + 1, 1)
+            one_block(b, 0)
+            fetch((b + 2) % blocks, 0)
+            one_block(b + 1, 1)
             return 0
 
-        lax.fori_loop(0, blocks, one_block, 0)
+        lax.fori_loop(0, blocks // 2, two_blocks, 0)
         return 0
 
     lax.fori_loop(0, group // batch, one_batch, 0)
@@ -296,12 +318,11 @@
     place = iota((cells, 1), 0)
     weights = jnp.zeros(lane.shape, f32)
     for n in range(9):
-        spot = jnp.zeros((cells, 1), jnp.int32)
         for b in range(cells):
             p = (b // by + n // 3) * wide + b % by + n % 3
-            spot = jnp.where(place == b, p, spot)
-        spot = spot + (dip_ref[:, n : n + 1] + DIP) * lag_rows
-        weights = weights + jnp.where(lane == spot, CENTER_WEIGHT if n == 4 else SIDE_WEIGHT, 0.0)
+            spot = p + (dip_ref[b // by, b % by, n] + DIP) * lag_rows
+            factor = CENTER_WEIGHT if n == 4 else SIDE_WEIGHT
+            weights = weights + jnp.where((place == b) & (lane == spot), factor, 0.0)
     weights = weights.astype(bf16)
     if lagged.shape[0] > lags * lag_rows:
         lagged[lags * lag_rows :, :] = jnp.zeros((lagged.shape[0] - lags * lag_rows, samples), f32)
@@ -370,13 +391,6 @@
     c.batch = 2
     cells = c.bx * c.by
     bins = c.nz * cells
-    base = (trace_owner % c.group) * c.rows + (trace_owner // c.group) * c.cap
-    zero = jnp.zeros((count,), f32)
-    meta = jnp.stack(
-        [trace_owner.astype(f32), base.astype(f32), trace_offset.astype(f32), (trace_cell + 1).astype(f32)]
-        + [zero] * 4
-    )
-    dips = dip_shift.reshape(9, cells).T
     samples = c.samples
     blocks = samples // LANES
     batch_rows = c.batch * c.rows
@@ -385,9 +399,15 @@
     return pl.pallas_call(
         functools.partial(kernel, c),
         out_shape=jax.ShapeDtypeStruct((c.bx, c.by, samples), f32),
-        in_specs=[pl.BlockSpec(memory_space=pltpu.VMEM)] * 5,
+        in_specs=[pl.BlockSpec(memory_space=pltpu.VMEM)] * 3
+        + [pl.BlockSpec(memory_space=pl.ANY)]
+        + [pl.BlockSpec(memory_space=pltpu.VMEM)] * 2
+        + [pl.BlockSpec(memory_space=pltpu.SMEM)],
         out_specs=pl.BlockSpec(memory_space=pltpu.VMEM),
         scratch_shapes=[
+            pltpu.VMEM((count, samples), bf16),
+            pltpu.VMEM((cells, samples), f32),
+            pltpu.VMEM((1, samples), jnp.int32),
             pltpu.VMEM((c.group, c.rows, samples), bf16),
             pltpu.VMEM((c.group, 16, c.meta_rows), bf16),
             pltpu.VMEM((c.group * c.rows, samples + LANES), bf16),
@@ -395,23 +415,23 @@
             pltpu.VMEM((c.nz, cells, samples), f32),
             pltpu.VMEM((4 * bins, samples), bf16),
             pltpu.VMEM((blocks, 2 * LANES, BAND * LANES), bf16),
-            pltpu.VMEM((batch_rows, BAND * LANES), f32),
-            pltpu.VMEM((batch_rows, LANES), f32),
+            pltpu.VMEM((2, batch_rows, BAND * LANES), f32),
+            pltpu.VMEM((2, batch_rows, LANES), f32),
             pltpu.VMEM((3, batch_rows, LANES), f32),
             pltpu.VMEM((c.nz, cells, samples + LANES), f32),
             pltpu.VMEM((c.nz - 1, cells, samples + LANES), f32),
             pltpu.VMEM((cells, samples), f32),
             pltpu.VMEM((8, cells, samples), f32),
             pltpu.VMEM((up_to((2 * DIP + 1) * lag_rows, LANES), samples), f32),
-            dma((c.group,)), dma((c.group,)), dma((c.group,)), dma((c.group,)),
+            dma, dma((c.group,)), dma((c.group,)), dma((c.group,)), dma((c.group,)),
             dma((c.nz,)), dma((c.nz,)), dma((c.nz,)), dma((c.nz,)),
             dma((8,)), dma((8,)),
         ],
         compiler_params=pltpu.CompilerParams(
-            collective_id=0, has_side_effects=True, vmem_limit_bytes=48 * 1024 * 1024
+            collective_id=0, has_side_effects=True, vmem_limit_bytes=56 * 1024 * 1024
         ),
         name="bin_stack_smooth",
-    )(meta, traces, slowness.reshape(cells, samples), band_start.reshape(1, samples), dips)
+    )(trace_owner, trace_offset, trace_cell, traces, slowness, band_start, dip_shift.transpose(1, 2, 0))
 
 
 def solution(mesh):

time: 61.3 us -> 50.7 us (0.83)
  the two profiles are of different devices: /device:TPU:12 before, /device:TPU:0 now
where the time goes in v2:
time: 50.7 us; the launch traced here: 50.1 us
  Pallas kernels  48.7 us (96%)
  local copies, waits for them, and re-layouts  1.42 us (3%)
    pallas_call x1, Pallas kernels, body(): pl.pallas_call(functools.partial(kernel, c), out_shape=jax.ShapeDtypeStru...  48.7 us
    unnamed x1, local copies, waits for them, and re-layouts  1.42 us

profile of v2, /device:TPU:0, one launch (start us, length us, event | category | flops | bytes accessed | tf_op | source)
XLA Modules:
  0.0 50.1 jit_solution(12721318359568629112)
XLA Ops:
  0.0 48.7 %bin_stack_smooth.1 = f32[2,4,1536]{2,1,0:T(4,128)} custom-call(s32[512]{0:T(512)} %owner_ref.1, bf16[512]{0:T(512)(128)(2,1)} %offset_ref.1, s32[512]{0:T(512)} %cell_ref.1, bf16[512,1536]{1,0:T(8,128)(2,1)} %traces_hbm.1, f32[2,4,1536]{2,1,0:T(4,128)} %slow_in.1, s32[1536]{0:T(1024)} %band_in.1, s32[2,4,9]{2,1,0:T(4,128)} %bitcast.1), custom_call_target="tpu_custom_call" | custom-call | tf_op jit(solution)/shard_map/bin_stack_smooth/pallas_call | solution.py:399
  48.7 1.4 %copy.9 = f32[2,4,1536]{2,1,0:T(4,128)} copy(f32[2,4,1536]{2,1,0:T(4,128)} %bin_stack_smooth.1) | data formatting | bytes 98304

commit v3 on v2

--- a/solution.py
+++ b/solution.py
@@ -43,7 +43,7 @@
 def kernel(
     c, owner_ref, offset_ref, cell_ref, traces_hbm, slow_in, band_in, dip_ref, out_ref,
     traces_ref, slow_ref, band_ref, send, send_meta, recv, recv_meta, slows, slow_parts, gather, picks, slow_rows, moved,
-    sums, sums_in, stack, halo, lagged,
+    sums, sums_in, padded, lagged,
     t_sem, s_send, s_recv, m_send, m_recv, w_send, w_recv, z_send, z_recv, h_send, h_recv,
 ):
     nx, nil, nz, group, cap, rows, samples = c.nx, c.nil, c.nz, c.group, c.cap, c.rows, c.samples
@@ -186,7 +186,21 @@
     batch_rows = batch * rows
     tile = 32 if batch_rows % 32 == 0 else 16
 
-    def one_batch(i, _):
+    pieces = c.pieces
+    per_piece = blocks // pieces
+
+    def piece_lanes(p):
+        first = 0 if p == 0 else LANES + p * per_piece * LANES
+        return pl.ds(first, LANES + (p + 1) * per_piece * LANES - first)
+
+    def sum_copy(k, p):
+        return pltpu.make_async_remote_copy(
+            src_ref=sums.at[(z + k) % nz, :, piece_lanes(p)], dst_ref=sums_in.at[k - 1, :, piece_lanes(p)],
+            send_sem=z_send.at[k * pieces + p], recv_sem=z_recv.at[k * pieces + p],
+            device_id=z_id(k), device_id_type=MESH,
+        )
+
+    def one_batch(i, last):
         for j in range(batch):
             k = i * batch + j
 
@@ -219,8 +233,8 @@
         turned = lax.dot_general(eye, members, NT_DIMS, preferred_element_type=f32)
         fold = jnp.sum(turned, axis=1, keepdims=True)
         turned = turned.astype(bf16)
-        last = pl.ds(samples, LANES)
-        sums[:, :, last] = sums[:, :, last] + jnp.broadcast_to(fold, (bins, LANES)).reshape(nz, cells, LANES)
+        head = pl.ds(0, LANES)
+        sums[:, :, head] = sums[:, :, head] + jnp.broadcast_to(fold, (bins, LANES)).reshape(nz, cells, LANES)
         offset2 = jnp.broadcast_to(offset * offset, (batch_rows, LANES))
         moved[2] = offset2
 
@@ -234,12 +248,13 @@
             lanes = pl.ds(start, LANES)
             time = (iota((1, LANES), 1) + start).astype(f32)
             time2 = time * time
-            center = band_ref[:, lanes].astype(f32) + 0.5 * (BAND - 1)
+            center = band_ref[:, lanes].astype(f32) + 0.5 * (BAND - 1) - time
 
             def one_tile(r, _):
                 here = pl.ds(pl.multiple_of(r * tile, 16), tile)
-                moveout = jnp.sqrt(time2 + moved[2, here, :] * slow_rows[at_slot, here, :])
-                off = center - moveout
+                delay2 = moved[2, here, :] * slow_rows[at_slot, here, :]
+                square = jnp.maximum(time2 + delay2, 1e-30)
+                off = center - delay2 * pl.reciprocal(time + square * lax.rsqrt(square), approx=True)
                 u = off * off
                 u2 = u * u
                 terms = []
@@ -257,13 +272,16 @@
                         merged.append((n1 * q2 + n2 * q1, v1 * q2 + v2 * q1, q))
                     terms = merged
                 n, v, _q = terms[0]
-                moved[at_slot, here, :] = n / (v + v)
+                v = v + v
+                inverse = pl.reciprocal(v, approx=True)
+                moved[at_slot, here, :] = n * (inverse * (2.0 - v * inverse))
                 return 0
 
             lax.fori_loop(0, batch_rows // tile, one_tile, 0, unroll=True)
             high, low = parts(moved[at_slot], 2)
             total = dot(turned, high) + dot(turned, low)
-            sums[:, :, lanes] = sums[:, :, lanes] + total.reshape(nz, cells, LANES)
+            after = pl.ds(pl.multiple_of(start + LANES, LANES), LANES)
+            sums[:, :, after] = sums[:, :, after] + total.reshape(nz, cells, LANES)
 
         fetch(0, 0)
 
@@ -275,42 +293,58 @@
             one_block(b + 1, 1)
             return 0
 
-        lax.fori_loop(0, blocks // 2, two_blocks, 0)
-        return 0
-
-    lax.fori_loop(0, group // batch, one_batch, 0)
-
-    def sum_copy(k):
-        return pltpu.make_async_remote_copy(
-            src_ref=sums.at[(z + k) % nz], dst_ref=sums_in.at[k - 1],
-            send_sem=z_send.at[k], recv_sem=z_recv.at[k], device_id=z_id(k), device_id_type=MESH,
-        )
-
-    lax.fori_loop(1, nz, lambda k, _: (sum_copy(k).start(), 0)[1], 0)
-    total = sums[pl.ds(z, 1)][0]
-    for k in range(1, nz):
-        sum_copy(k).wait_recv()
-        total = total + sums_in[k - 1]
-    stack[...] = total[:, :samples] / jnp.maximum(total[:, samples : samples + 1], 1.0)
-
-    def halo_copy(i, dx, dy):
-        return pltpu.make_async_remote_copy(
-            src_ref=stack, dst_ref=halo.at[len(around) - 1 - i],
-            send_sem=h_send.at[i], recv_sem=h_recv.at[len(around) - 1 - i],
-            device_id=near_id(dx, dy), device_id_type=MESH,
-        )
-
-    def halo_wait(i):
-        return pltpu.make_async_remote_copy(
-            src_ref=stack, dst_ref=halo.at[i], send_sem=h_send.at[i], recv_sem=h_recv.at[i],
-            device_id=near_id(*around[i]), device_id_type=MESH,
-        )
-
-    for i, (dx, dy) in enumerate(around):
-        pl.when(valid(dx, dy))(functools.partial(lambda i, dx, dy: halo_copy(i, dx, dy).start(), i, dx, dy))
+        if not last:
+            lax.fori_loop(0, blocks // 2, two_blocks, 0)
+            return 0
+        for p in range(pieces):
+            lax.fori_loop(p * per_piece // 2, (p + 1) * per_piece // 2, two_blocks, 0)
+            for k in range(1, nz):
+                sum_copy(k, p).start()
+
+    lax.fori_loop(0, group // batch - 1, lambda i, _: one_batch(i, False), 0)
+    one_batch(group // batch - 1, True)
 
     bx, by = c.bx, c.by
     wide = by + 2
+
+    def strips(dx, dy):
+        rows_x = range(bx) if dx == 0 else [bx - 1 if dx == 1 else 0]
+        row_y, run = (0, by) if dy == 0 else (by - 1 if dy == 1 else 0, 1)
+        return [
+            ((row + 1) * wide + row_y + 1, (row + 1 - dx * bx) * wide + row_y + 1 - dy * by, run) for row in rows_x
+        ]
+
+    strip_list = [(dx, dy) + strip for dx, dy in around for strip in strips(dx, dy)]
+
+    def halo_copy(j, p, way=1):
+        dx, dy, source, target, run = strip_list[j]
+        lanes = pl.ds(p * per_piece * LANES, per_piece * LANES)
+        return pltpu.make_async_remote_copy(
+            src_ref=padded.at[pl.ds(source, run), :, lanes], dst_ref=padded.at[pl.ds(target, run), :, lanes],
+            send_sem=h_send.at[j * pieces + p], recv_sem=h_recv.at[j * pieces + p],
+            device_id=near_id(way * dx, way * dy), device_id_type=MESH,
+        )
+
+    fold = None
+    for p in range(pieces):
+        total = sums[pl.ds(z, 1), :, piece_lanes(p)][0]
+        for k in range(1, nz):
+            sum_copy(k, p).wait_recv()
+            total = total + sums_in[k - 1, :, piece_lanes(p)]
+        if p == 0:
+            fold = jnp.maximum(total[:, :1], 1.0)
+            total = total[:, LANES:]
+        total = total / fold
+        for b in range(cells):
+            padded[(b // by + 1) * wide + b % by + 1, :, p * per_piece * LANES : (p + 1) * per_piece * LANES] = total[b : b + 1]
+        for dx, dy in around:
+
+            @pl.when(valid(dx, dy))
+            def _():
+                for j, strip in enumerate(strip_list):
+                    if strip[:2] == (dx, dy):
+                        halo_copy(j, p).start()
+
     padded_rows = (bx + 2) * wide
     lag_rows = up_to(padded_rows, 8)
     lags = 2 * DIP + 1
@@ -327,28 +361,29 @@
     if lagged.shape[0] > lags * lag_rows:
         lagged[lags * lag_rows :, :] = jnp.zeros((lagged.shape[0] - lags * lag_rows, samples), f32)
 
-    for i, (dx, dy) in enumerate(around):
-        ok = valid(dx, dy)
-        pl.when(ok)(functools.partial(lambda i: halo_wait(i).wait_recv(), i))
+    for dx, dy in around:
+        ok = valid(-dx, -dy)
+        mine_in = [j for j, strip in enumerate(strip_list) if strip[:2] == (dx, dy)]
+
+        @pl.when(ok)
+        def _():
+            for j in mine_in:
+                for p in range(pieces):
+                    halo_copy(j, p, -1).wait_recv()
 
         @pl.when(jnp.logical_not(ok))
         def _():
-            halo[i] = jnp.zeros((cells, samples), f32)
-
-    lines = []
-    for px in range(bx + 2):
-        for py in range(wide):
-            dx = -1 if px == 0 else (1 if px == bx + 1 else 0)
-            dy = -1 if py == 0 else (1 if py == wide - 1 else 0)
-            line = (px - 1 - dx * bx) * by + (py - 1 - dy * by)
-            block = stack if (dx, dy) == (0, 0) else halo.at[around.index((dx, dy))]
-            lines.append(block[line : line + 1, :])
+            for j in mine_in:
+                target, run = strip_list[j][3:]
+                padded[pl.ds(target, run)] = jnp.zeros((run, 1, samples), f32)
+
+    lines = [padded[line] for line in range(padded_rows)]
     lines += [jnp.zeros((1, samples), f32)] * (lag_rows - padded_rows)
-    padded = jnp.concatenate(lines, axis=0)
+    whole = jnp.concatenate(lines, axis=0)
     time = iota((lag_rows, samples), 1)
     for i in range(lags):
         lag = i - DIP
-        shifted = padded if lag == 0 else pltpu.roll(padded, (-lag) % samples, 1)
+        shifted = whole if lag == 0 else pltpu.roll(whole, (-lag) % samples, 1)
         inside = (time + lag >= 0) & (time + lag < samples)
         lagged[i * lag_rows : (i + 1) * lag_rows, :] = jnp.where(inside, shifted, 0.0)
     result = sum(dot(weights, piece) for piece in parts(lagged[...], 3))
@@ -362,13 +397,20 @@
 
     def done_z(k, _):
         slow_copy(k).wait_send()
-        sum_copy(k).wait_send()
+        for p in range(pieces):
+            sum_copy(k, p).wait_send()
         return 0
 
     lax.fori_loop(1, group, done_plane, 0)
     lax.fori_loop(1, nz, done_z, 0)
-    for i, (dx, dy) in enumerate(around):
-        pl.when(valid(dx, dy))(functools.partial(lambda i, dx, dy: halo_copy(i, dx, dy).wait_send(), i, dx, dy))
+    for dx, dy in around:
+
+        @pl.when(valid(dx, dy))
+        def _():
+            for j, strip in enumerate(strip_list):
+                if strip[:2] == (dx, dy):
+                    for p in range(pieces):
+                        halo_copy(j, p).wait_send()
 
 
 class Sizes:
@@ -389,6 +431,7 @@
     c.meta_rows = up_to(c.rows, LANES)
     c.bx, c.by = slowness.shape[:2]
     c.batch = 2
+    c.pieces = 3
     cells = c.bx * c.by
     bins = c.nz * cells
     samples = c.samples
@@ -396,6 +439,7 @@
     batch_rows = c.batch * c.rows
     lag_rows = up_to((c.bx + 2) * (c.by + 2), 8)
     dma = pltpu.SemaphoreType.DMA
+    strip_count = 2 + 2 * c.bx + 4
     return pl.pallas_call(
         functools.partial(kernel, c),
         out_shape=jax.ShapeDtypeStruct((c.bx, c.by, samples), f32),
@@ -420,12 +464,11 @@
             pltpu.VMEM((3, batch_rows, LANES), f32),
             pltpu.VMEM((c.nz, cells, samples + LANES), f32),
             pltpu.VMEM((c.nz - 1, cells, samples + LANES), f32),
-            pltpu.VMEM((cells, samples), f32),
-            pltpu.VMEM((8, cells, samples), f32),
+            pltpu.VMEM(((c.bx + 2) * (c.by + 2), 1, samples), f32),
             pltpu.VMEM((up_to((2 * DIP + 1) * lag_rows, LANES), samples), f32),
             dma, dma((c.group,)), dma((c.group,)), dma((c.group,)), dma((c.group,)),
-            dma((c.nz,)), dma((c.nz,)), dma((c.nz,)), dma((c.nz,)),
-            dma((8,)), dma((8,)),
+            dma((c.nz,)), dma((c.nz,)), dma((c.nz * c.pieces,)), dma((c.nz * c.pieces,)),
+            dma((strip_count * c.pieces,)), dma((strip_count * c.pieces,)),
         ],
         compiler_params=pltpu.CompilerParams(
             collective_id=0, has_side_effects=True, vmem_limit_bytes=56 * 1024 * 1024

time: 50.7 us -> 47 us (0.927)
  Pallas kernels: 48.7 us -> 44.9 us
    pallas_call x1, Pallas kernels: 48.7 us -> 44.9 us  [body(): pl.pallas_call(functools.partial(kernel, c), out_shape=jax.ShapeDtypeStru...]
where the time goes in v3:
time: 47 us; the launch traced here: 46.3 us
  Pallas kernels  44.9 us (96%)
  local copies, waits for them, and re-layouts  1.42 us (3%)
    pallas_call x1, Pallas kernels, body(): pl.pallas_call(functools.partial(kernel, c), out_shape=jax.ShapeDtypeStru...  44.9 us
    unnamed x1, local copies, waits for them, and re-layouts  1.42 us

profile of v3, /device:TPU:0, one launch (start us, length us, event | category | flops | bytes accessed | tf_op | source)
XLA Modules:
  0.0 46.3 jit_solution(4899616782431938180)
XLA Ops:
  0.0 44.9 %bin_stack_smooth.1 = f32[2,4,1536]{2,1,0:T(4,128)} custom-call(s32[512]{0:T(512)} %owner_ref.1, bf16[512]{0:T(512)(128)(2,1)} %offset_ref.1, s32[512]{0:T(512)} %cell_ref.1, bf16[512,1536]{1,0:T(8,128)(2,1)} %traces_hbm.1, f32[2,4,1536]{2,1,0:T(4,128)} %slow_in.1, s32[1536]{0:T(1024)} %band_in.1, s32[2,4,9]{2,1,0:T(4,128)} %bitcast.1), custom_call_target="tpu_custom_call" | custom-call | tf_op jit(solution)/shard_map/bin_stack_smooth/pallas_call | solution.py:443
  44.9 1.4 %copy.9 = f32[2,4,1536]{2,1,0:T(4,128)} copy(f32[2,4,1536]{2,1,0:T(4,128)} %bin_stack_smooth.1) | data formatting | bytes 98304

commit v4 on v3

--- a/solution.py
+++ b/solution.py
@@ -48,6 +48,10 @@
 ):
     nx, nil, nz, group, cap, rows, samples = c.nx, c.nil, c.nz, c.group, c.cap, c.rows, c.samples
     ny = nil // 2
+    ring = c.ring
+    half = samples // 2
+    cols = half + LANES
+    half_blocks = half // LANES
     blocks = samples // LANES
     cells = slow_ref.shape[0]
     xl = lax.axis_index("xline")
@@ -55,18 +59,28 @@
     z, x = xl // nx, xl % nx
     y, core = il // 2, il % 2
 
-    def plane(k):
-        kx, ky, kc = k // nil, (k % nil) // 2, k % 2
-        tx = (x + kx) % nx
-        ti = ((y + ky) % ny) * 2 + (core + kc) % 2
-        return tx, ti
-
-    def plane_id(k):
-        tx, ti = plane(k)
-        return {"xline": z * nx + tx, "iline": ti}
-
-    def z_id(k):
-        return {"xline": ((z + k) % nz) * nx + x, "iline": il}
+    def plane(h, k):
+        tx = (x + (1 - h) * (k // 2)) % nx
+        ty = (y + h * (k // 2)) % ny
+        return tx, ty, (core + k % 2) % 2
+
+    def plane_id(h, k):
+        tx, ty, tc = plane(h, k)
+        return {"xline": z * nx + tx, "iline": ty * 2 + tc}
+
+    def column(h, k):
+        tz = (z + k // nx) % nz
+        tx = (x + h * (k % nx)) % nx
+        ty = (y + (1 - h) * (k % nx)) % ny
+        return tz, tx, ty
+
+    def column_id(h, k):
+        tz, tx, ty = column(h, k)
+        return {"xline": tz * nx + tx, "iline": ty * 2 + core}
+
+    def place_of(h, k):
+        tz, tx, ty = column(h, k)
+        return tz * nx + (1 - h) * ty + h * tx
 
     around = [(dx, dy) for dx in (-1, 0, 1) for dy in (-1, 0, 1) if (dx, dy) != (0, 0)]
 
@@ -89,8 +103,9 @@
     def greet(target):
         pl.semaphore_signal(barrier, inc=1, device_id=target, device_id_type=MESH)
 
-    lax.fori_loop(1, group, lambda k, _: (greet(plane_id(k)), 0)[1], 0)
-    lax.fori_loop(1, nz, lambda k, _: (greet(z_id(k)), 0)[1], 0)
+    for h in range(2):
+        lax.fori_loop(1, group, lambda k, _: (greet(plane_id(h, k)), 0)[1], 0)
+        lax.fori_loop(1, ring, lambda k, _: (greet(column_id(h, k)), 0)[1], 0)
     for dx, dy in around:
         pl.when(valid(dx, dy))(functools.partial(lambda t: greet(t), near_id(dx, dy)))
 
@@ -99,65 +114,84 @@
         slow_ref[line * c.by : (line + 1) * c.by, :] = slow_in[line]
     band_ref[...] = band_in[...].reshape(1, samples)
     owner_row = owner_ref[...].reshape(1, count).astype(f32)
-    turn = jnp.floor((owner_row + 0.5) * (1.0 / group))
-    base_row = (owner_row - turn * group) * rows + turn * cap
+
+    def split(value, size):
+        quotient = jnp.floor((value + 0.5) * (1.0 / size))
+        return quotient, value - quotient * size
+
+    owner_xl, owner_il = split(owner_row, nil)
+    owner_z, owner_x = split(owner_xl, nx)
+    owner_y, owner_core = split(owner_il, 2)
+    bases = [
+        (owner_x * 2.0 + owner_core) * rows + (owner_z * nx + owner_y) * cap,
+        (owner_y * 2.0 + owner_core) * rows + (owner_z * nx + owner_x) * cap,
+    ]
     offset_row = offset_ref[...].astype(f32).reshape(1, count)
     cell_row = cell_ref[...].reshape(1, count).astype(f32) + 1.0
-    owners = up_to(group * nz, 16)
+    owners = up_to(group * ring, 16)
     mine = jnp.where(iota((owners, count), 0).astype(f32) == owner_row, 1.0, 0.0)
     earlier = jnp.where(iota((count, count), 0) < iota((count, count), 1), 1.0, 0.0).astype(bf16)
     before = dot(mine.astype(bf16), earlier)
-    slot = base_row + jnp.sum(mine * before, axis=0, keepdims=True)
+    rank = jnp.sum(mine * before, axis=0, keepdims=True)
+    slots = [base + rank for base in bases]
     values = jnp.concatenate([offset_row, cell_row, jnp.zeros((14, count), f32)], axis=0).astype(bf16)
 
     def span_of(at, size):
         return 3 - jnp.where(at == 0, 1, 0) - jnp.where(at == size - 1, 1, 0)
 
     near = span_of(xl, nx * nz) * span_of(il, nil) - 1
-    pl.semaphore_wait(barrier, (group - 1) + (nz - 1) + near)
-
-    def slow_copy(k):
+    pl.semaphore_wait(barrier, 2 * (group - 1) + 2 * (ring - 1) + near)
+
+    def slow_copy(h, k):
         return pltpu.make_async_remote_copy(
-            src_ref=slow_ref, dst_ref=slows.at[z], send_sem=w_send.at[k], recv_sem=w_recv.at[k],
-            device_id=z_id(k), device_id_type=MESH,
+            src_ref=slow_ref.at[:, pl.ds(h * half, half)], dst_ref=slows.at[h, place_of(h, 0)],
+            send_sem=w_send.at[h * ring + k], recv_sem=w_recv.at[h * ring + k],
+            device_id=column_id(h, k), device_id_type=MESH,
         )
 
-    def row_copy(k):
+    def row_copy(h, k):
+        n = h * group + k
         return pltpu.make_async_remote_copy(
-            src_ref=send.at[k], dst_ref=recv.at[pl.ds(pl.multiple_of(k * rows, 16), rows), pl.ds(0, samples)],
-            send_sem=s_send.at[k], recv_sem=s_recv.at[k], device_id=plane_id(k), device_id_type=MESH,
+            src_ref=send.at[n], dst_ref=recv.at[pl.ds(pl.multiple_of(n * rows, 16), rows)],
+            send_sem=s_send.at[n], recv_sem=s_recv.at[n], device_id=plane_id(h, k), device_id_type=MESH,
         )
 
-    def meta_copy(k):
+    def meta_copy(h, k):
+        n = h * group + k
         return pltpu.make_async_remote_copy(
-            src_ref=send_meta.at[k], dst_ref=recv_meta.at[k],
-            send_sem=m_send.at[k], recv_sem=m_recv.at[k], device_id=plane_id(k), device_id_type=MESH,
+            src_ref=send_meta.at[n], dst_ref=recv_meta.at[n],
+            send_sem=m_send.at[n], recv_sem=m_recv.at[n], device_id=plane_id(h, k), device_id_type=MESH,
         )
 
-    lax.fori_loop(1, nz, lambda k, _: (slow_copy(k).start(), 0)[1], 0)
-
-    def pack(k):
-        tx, ti = plane(k)
-        first = ((tx * nil + ti) * rows).astype(f32)
-        hot = jnp.where(iota((c.meta_rows, count), 0).astype(f32) + first == slot, 1.0, 0.0).astype(bf16)
-        chunk = dot(hot[:rows], traces_ref[...])
-        chunk = pltpu.roll(chunk, LANES // 2, 1).astype(bf16)
+    for h in range(2):
+        lax.fori_loop(1, ring, lambda k, _: (slow_copy(h, k).start(), 0)[1], 0)
+
+    def pack(h, k):
+        tx, ty, tc = plane(h, k)
+        first = (((ty if h else tx) * 2 + tc) * rows).astype(f32)
+        hot = jnp.where(iota((c.meta_rows, count), 0).astype(f32) + first == slots[h], 1.0, 0.0).astype(bf16)
+        start = h * (samples - cols)
+        chunk = dot(hot[:rows], traces_ref[:, start : start + cols])
+        chunk = pltpu.roll(chunk, cols - LANES // 2 if h else LANES // 2, 1).astype(bf16)
         info = lax.dot_general(values, hot, NT_DIMS, preferred_element_type=f32).astype(bf16)
         return chunk, info
 
-    def send_one(k, _):
-        chunk, info = pack(k)
-        send[k] = chunk
-        send_meta[k] = info
-        meta_copy(k).start()
-        row_copy(k).start()
+    def send_one(j, _):
+        k = j % (group - 1) + 1
+        for h in range(2):
+            chunk, info = pack(h, k)
+            send[h * group + k] = chunk
+            send_meta[h * group + k] = info
+            meta_copy(h, k).start()
+            row_copy(h, k).start()
         return 0
 
     traces_copy.wait()
     lax.fori_loop(1, group, send_one, 0)
-    chunk, info = pack(0)
-    recv[0:rows, 0:samples] = chunk
-    recv_meta[0] = info
+    for h in range(2):
+        chunk, info = pack(h, 0)
+        recv[h * group * rows : (h * group + 1) * rows, :] = chunk
+        recv_meta[h * group] = info
 
     def make_gather(b, _):
         start = pl.multiple_of(b * LANES, LANES)
@@ -173,59 +207,59 @@
 
     lax.fori_loop(0, blocks, make_gather, 0)
 
-    slows[pl.ds(z, 1)] = slow_ref[...][None]
-    lax.fori_loop(1, nz, lambda k, _: (slow_copy(k).wait_recv(), 0)[1], 0)
-    bins = nz * cells
-    table = slows[...].reshape(bins, samples)
-    for i, piece in enumerate(parts(table, 3)):
-        slow_parts[i * bins : (i + 1) * bins, :] = piece
-    slow_parts[3 * bins :, :] = jnp.zeros((bins, samples), bf16)
+    bins = ring * cells
+    for h in range(2):
+        slows[h, pl.ds(place_of(h, 0), 1)] = slow_ref[:, h * half : (h + 1) * half][None]
+        lax.fori_loop(1, ring, lambda k, _: (slow_copy(h, k).wait_recv(), 0)[1], 0)
+        table = slows[h].reshape(bins, half)
+        for i, piece in enumerate(parts(table, 3)):
+            slow_parts[h, i * bins : (i + 1) * bins, :] = piece
+        slow_parts[h, 3 * bins :, :] = jnp.zeros((bins, half), bf16)
 
     sums[...] = jnp.zeros_like(sums)
-    batch = c.batch
-    batch_rows = batch * rows
-    tile = 32 if batch_rows % 32 == 0 else 16
-
-    pieces = c.pieces
-    per_piece = blocks // pieces
-
-    def piece_lanes(p):
+    tile = 32 if rows % 32 == 0 else 16
+    counts = c.counts
+
+    def piece_lanes(h, p):
+        per_piece = half_blocks // counts[h]
         first = 0 if p == 0 else LANES + p * per_piece * LANES
         return pl.ds(first, LANES + (p + 1) * per_piece * LANES - first)
 
-    def sum_copy(k, p):
+    def piece_id(h, p):
+        return h * counts[0] + p
+
+    pieces = sum(counts)
+    piece_list = [(h, p) for h in range(2) for p in range(counts[h])]
+
+    def sum_copy(h, p, k):
+        n = piece_id(h, p) * ring + k
         return pltpu.make_async_remote_copy(
-            src_ref=sums.at[(z + k) % nz, :, piece_lanes(p)], dst_ref=sums_in.at[k - 1, :, piece_lanes(p)],
-            send_sem=z_send.at[k * pieces + p], recv_sem=z_recv.at[k * pieces + p],
-            device_id=z_id(k), device_id_type=MESH,
+            src_ref=sums.at[h, place_of(h, k), :, piece_lanes(h, p)], dst_ref=sums_in.at[h, k - 1, :, piece_lanes(h, p)],
+            send_sem=z_send.at[n], recv_sem=z_recv.at[n],
+            device_id=column_id(h, k), device_id_type=MESH,
         )
 
-    def one_batch(i, last):
-        for j in range(batch):
-            k = i * batch + j
-
-            @pl.when(k > 0)
-            def _():
-                meta_copy(k).wait_recv()
-                row_copy(k).wait_recv()
-
-        span = pl.ds(pl.multiple_of(i * batch_rows, 16), batch_rows)
-        recv[span, samples : samples + LANES] = recv[span, 0:LANES]
+    def send_sums(h, p):
+        lax.fori_loop(1, ring, lambda k, _: (sum_copy(h, p, k).start(), 0)[1], 0)
+
+    def one_batch(h, k, last):
+        n = h * group + k
+
+        @pl.when(k > 0)
+        def _():
+            meta_copy(h, k).wait_recv()
+            row_copy(h, k).wait_recv()
+
+        span = pl.ds(pl.multiple_of(n * rows, 16), rows)
+        batch_rows = rows
         same = jnp.where(iota((rows, c.meta_rows), 0) == iota((rows, c.meta_rows), 1), 1.0, 0.0).astype(bf16)
-        columns = jnp.concatenate(
-            [
-                lax.dot_general(same, recv_meta[i * batch + j], NT_DIMS, preferred_element_type=f32)
-                for j in range(batch)
-            ],
-            axis=0,
-        )
+        columns = lax.dot_general(same, recv_meta[n], NT_DIMS, preferred_element_type=f32)
         offset = columns[:, 0:1]
         cell = columns[:, 1:2]
         step = iota((batch_rows, 1), 0)
         base = jnp.zeros((batch_rows, 1), f32)
-        for j in range(batch):
-            for owner in range(1, nz):
-                base = base + jnp.where((step >= j * rows + owner * cap) & (step < (j + 1) * rows), float(cells), 0.0)
+        for owner in range(1, ring):
+            base = base + jnp.where(step >= owner * cap, float(cells), 0.0)
         bin_id = jnp.where(cell > 0.5, base + cell - 1.0, -1.0)
         lane = iota((1, 4 * bins), 1)
         members = jnp.where((lane % bins).astype(f32) == bin_id, 1.0, 0.0).astype(bf16)
@@ -234,19 +268,20 @@
         fold = jnp.sum(turned, axis=1, keepdims=True)
         turned = turned.astype(bf16)
         head = pl.ds(0, LANES)
-        sums[:, :, head] = sums[:, :, head] + jnp.broadcast_to(fold, (bins, LANES)).reshape(nz, cells, LANES)
+        sums[h, :, :, head] = sums[h, :, :, head] + jnp.broadcast_to(fold, (bins, LANES)).reshape(ring, cells, LANES)
         offset2 = jnp.broadcast_to(offset * offset, (batch_rows, LANES))
         moved[2] = offset2
 
         def fetch(b, at):
             start = pl.multiple_of(b * LANES, LANES)
-            picks[at] = dot(recv[span, pl.ds(start, 2 * LANES)], gather[b])
-            slow_rows[at] = dot(members, slow_parts[:, pl.ds(start, LANES)])
+            picks[at] = dot(recv[span, pl.ds(start, 2 * LANES)], gather[h * half_blocks + b])
+            slow_rows[at] = dot(members, slow_parts[h, :, pl.ds(start, LANES)])
 
         def one_block(b, at_slot):
             start = pl.multiple_of(b * LANES, LANES)
-            lanes = pl.ds(start, LANES)
-            time = (iota((1, LANES), 1) + start).astype(f32)
+            here_start = pl.multiple_of(start + h * half, LANES)
+            lanes = pl.ds(here_start, LANES)
+            time = (iota((1, LANES), 1) + here_start).astype(f32)
             time2 = time * time
             center = band_ref[:, lanes].astype(f32) + 0.5 * (BAND - 1) - time
 
@@ -281,7 +316,7 @@
             high, low = parts(moved[at_slot], 2)
             total = dot(turned, high) + dot(turned, low)
             after = pl.ds(pl.multiple_of(start + LANES, LANES), LANES)
-            sums[:, :, after] = sums[:, :, after] + total.reshape(nz, cells, LANES)
+            sums[h, :, :, after] = sums[h, :, :, after] + total.reshape(ring, cells, LANES)
 
         fetch(0, 0)
 
@@ -289,20 +324,24 @@
             b = 2 * i
             fetch(b + 1, 1)
             one_block(b, 0)
-            fetch((b + 2) % blocks, 0)
+            fetch((b + 2) % half_blocks, 0)
             one_block(b + 1, 1)
             return 0
 
         if not last:
-            lax.fori_loop(0, blocks // 2, two_blocks, 0)
+            lax.fori_loop(0, half_blocks // 2, two_blocks, 0)
             return 0
-        for p in range(pieces):
+        per_piece = half_blocks // counts[h]
+        for p in range(counts[h]):
             lax.fori_loop(p * per_piece // 2, (p + 1) * per_piece // 2, two_blocks, 0)
-            for k in range(1, nz):
-                sum_copy(k, p).start()
-
-    lax.fori_loop(0, group // batch - 1, lambda i, _: one_batch(i, False), 0)
-    one_batch(group // batch - 1, True)
+            send_sums(h, p)
+
+    lax.fori_loop(0, 4, lambda i, _: one_batch(i % 2, i // 2, False), 0)
+    lax.fori_loop(2, group, lambda k, _: one_batch(0, k, False), 0)
+    for p in range(counts[0]):
+        send_sums(0, p)
+    lax.fori_loop(2, group - 1, lambda k, _: one_batch(1, k, False), 0)
+    one_batch(1, group - 1, True)
 
     bx, by = c.bx, c.by
     wide = by + 2
@@ -316,34 +355,39 @@
 
     strip_list = [(dx, dy) + strip for dx, dy in around for strip in strips(dx, dy)]
 
-    def halo_copy(j, p, way=1):
+    def piece_span(h, p):
+        per_piece = half // counts[h]
+        return h * half + p * per_piece, per_piece
+
+    def halo_copy(j, n, way=1):
         dx, dy, source, target, run = strip_list[j]
-        lanes = pl.ds(p * per_piece * LANES, per_piece * LANES)
+        lanes = pl.ds(*piece_span(*piece_list[n]))
         return pltpu.make_async_remote_copy(
             src_ref=padded.at[pl.ds(source, run), :, lanes], dst_ref=padded.at[pl.ds(target, run), :, lanes],
-            send_sem=h_send.at[j * pieces + p], recv_sem=h_recv.at[j * pieces + p],
+            send_sem=h_send.at[j * pieces + n], recv_sem=h_recv.at[j * pieces + n],
             device_id=near_id(way * dx, way * dy), device_id_type=MESH,
         )
 
-    fold = None
-    for p in range(pieces):
-        total = sums[pl.ds(z, 1), :, piece_lanes(p)][0]
-        for k in range(1, nz):
-            sum_copy(k, p).wait_recv()
-            total = total + sums_in[k - 1, :, piece_lanes(p)]
+    folds = [None, None]
+    for n, (h, p) in enumerate(piece_list):
+        total = sums[h, pl.ds(place_of(h, 0), 1), :, piece_lanes(h, p)][0]
+        for k in range(1, ring):
+            sum_copy(h, p, k).wait_recv()
+            total = total + sums_in[h, k - 1, :, piece_lanes(h, p)]
         if p == 0:
-            fold = jnp.maximum(total[:, :1], 1.0)
+            folds[h] = jnp.maximum(total[:, :1], 1.0)
             total = total[:, LANES:]
-        total = total / fold
+        total = total / folds[h]
+        first, size = piece_span(h, p)
         for b in range(cells):
-            padded[(b // by + 1) * wide + b % by + 1, :, p * per_piece * LANES : (p + 1) * per_piece * LANES] = total[b : b + 1]
+            padded[(b // by + 1) * wide + b % by + 1, :, first : first + size] = total[b : b + 1]
         for dx, dy in around:
 
             @pl.when(valid(dx, dy))
             def _():
                 for j, strip in enumerate(strip_list):
                     if strip[:2] == (dx, dy):
-                        halo_copy(j, p).start()
+                        halo_copy(j, n).start()
 
     padded_rows = (bx + 2) * wide
     lag_rows = up_to(padded_rows, 8)
@@ -391,18 +435,20 @@
         out_ref[row] = result[row * by : (row + 1) * by, :]
 
     def done_plane(k, _):
-        meta_copy(k).wait_send()
-        row_copy(k).wait_send()
+        for h in range(2):
+            meta_copy(h, k).wait_send()
+            row_copy(h, k).wait_send()
         return 0
 
-    def done_z(k, _):
-        slow_copy(k).wait_send()
-        for p in range(pieces):
-            sum_copy(k, p).wait_send()
+    def done_column(k, _):
+        for h in range(2):
+            slow_copy(h, k).wait_send()
+        for h, p in piece_list:
+            sum_copy(h, p, k).wait_send()
         return 0
 
     lax.fori_loop(1, group, done_plane, 0)
-    lax.fori_loop(1, nz, done_z, 0)
+    lax.fori_loop(1, ring, done_column, 0)
     for dx, dy in around:
 
         @pl.when(valid(dx, dy))
@@ -424,19 +470,23 @@
     while c.nz * c.nz < size_x:
         c.nz *= 2
     c.nx = size_x // c.nz
-    c.group = c.nx * c.nil
+    assert c.nx * 2 == c.nil
+    c.group = c.nil
+    c.ring = c.nz * c.nx
     count, c.samples = traces.shape
     c.cap = max(2, 5 * count // (4 * size_x * c.nil))
-    c.rows = up_to(c.nz * c.cap, 16)
+    c.rows = up_to(c.ring * c.cap, 16)
     c.meta_rows = up_to(c.rows, LANES)
     c.bx, c.by = slowness.shape[:2]
-    c.batch = 2
-    c.pieces = 3
+    c.counts = (1, 3)
     cells = c.bx * c.by
-    bins = c.nz * cells
+    bins = c.ring * cells
     samples = c.samples
     blocks = samples // LANES
-    batch_rows = c.batch * c.rows
+    batch_rows = c.rows
+    half = samples // 2
+    cols = half + LANES
+    pieces = sum(c.counts)
     lag_rows = up_to((c.bx + 2) * (c.by + 2), 8)
     dma = pltpu.SemaphoreType.DMA
     strip_count = 2 + 2 * c.bx + 4
@@ -452,23 +502,23 @@
             pltpu.VMEM((count, samples), bf16),
             pltpu.VMEM((cells, samples), f32),
             pltpu.VMEM((1, samples), jnp.int32),
-            pltpu.VMEM((c.group, c.rows, samples), bf16),
-            pltpu.VMEM((c.group, 16, c.meta_rows), bf16),
-            pltpu.VMEM((c.group * c.rows, samples + LANES), bf16),
-            pltpu.VMEM((c.group, 16, c.meta_rows), bf16),
-            pltpu.VMEM((c.nz, cells, samples), f32),
-            pltpu.VMEM((4 * bins, samples), bf16),
+            pltpu.VMEM((2 * c.group, c.rows, cols), bf16),
+            pltpu.VMEM((2 * c.group, 16, c.meta_rows), bf16),
+            pltpu.VMEM((2 * c.group * c.rows, cols), bf16),
+            pltpu.VMEM((2 * c.group, 16, c.meta_rows), bf16),
+            pltpu.VMEM((2, c.ring, cells, half), f32),
+            pltpu.VMEM((2, 4 * bins, half), bf16),
             pltpu.VMEM((blocks, 2 * LANES, BAND * LANES), bf16),
             pltpu.VMEM((2, batch_rows, BAND * LANES), f32),
             pltpu.VMEM((2, batch_rows, LANES), f32),
             pltpu.VMEM((3, batch_rows, LANES), f32),
-            pltpu.VMEM((c.nz, cells, samples + LANES), f32),
-            pltpu.VMEM((c.nz - 1, cells, samples + LANES), f32),
+            pltpu.VMEM((2, c.ring, cells, cols), f32),
+            pltpu.VMEM((2, c.ring - 1, cells, cols), f32),
             pltpu.VMEM(((c.bx + 2) * (c.by + 2), 1, samples), f32),
             pltpu.VMEM((up_to((2 * DIP + 1) * lag_rows, LANES), samples), f32),
-            dma, dma((c.group,)), dma((c.group,)), dma((c.group,)), dma((c.group,)),
-            dma((c.nz,)), dma((c.nz,)), dma((c.nz * c.pieces,)), dma((c.nz * c.pieces,)),
-            dma((strip_count * c.pieces,)), dma((strip_count * c.pieces,)),
+            dma, dma((2 * c.group,)), dma((2 * c.group,)), dma((2 * c.group,)), dma((2 * c.group,)),
+            dma((2 * c.ring,)), dma((2 * c.ring,)), dma((pieces * c.ring,)), dma((pieces * c.ring,)),
+            dma((strip_count * pieces,)), dma((strip_count * pieces,)),
         ],
         compiler_params=pltpu.CompilerParams(
             collective_id=0, has_side_effects=True, vmem_limit_bytes=56 * 1024 * 1024

time: 47 us -> 51.5 us (1.096)
  Pallas kernels: 44.9 us -> 49.8 us
    pallas_call x1, Pallas kernels: 44.9 us -> 49.8 us  [body(): pl.pallas_call(functools.partial(kernel, c), out_shape=jax.ShapeDtypeStru...]
where the time goes in v4:
time: 51.5 us; the launch traced here: 51.3 us
  Pallas kernels  49.8 us (97%)
  local copies, waits for them, and re-layouts  1.42 us (3%)
    pallas_call x1, Pallas kernels, body(): pl.pallas_call(functools.partial(kernel, c), out_shape=jax.ShapeDtypeStru...  49.8 us
    unnamed x1, local copies, waits for them, and re-layouts  1.42 us

profile of v4, /device:TPU:0, one launch (start us, length us, event | category | flops | bytes accessed | tf_op | source)
XLA Modules:
  0.0 51.3 jit_solution(6114278807660306430)
XLA Ops:
  0.0 49.8 %bin_stack_smooth.1 = f32[2,4,1536]{2,1,0:T(4,128)} custom-call(s32[512]{0:T(512)} %owner_ref.1, bf16[512]{0:T(512)(128)(2,1)} %offset_ref.1, s32[512]{0:T(512)} %cell_ref.1, bf16[512,1536]{1,0:T(8,128)(2,1)} %traces_hbm.1, f32[2,4,1536]{2,1,0:T(4,128)} %slow_in.1, s32[1536]{0:T(1024)} %band_in.1, s32[2,4,9]{2,1,0:T(4,128)} %bitcast.1), custom_call_target="tpu_custom_call" | custom-call | tf_op jit(solution)/shard_map/bin_stack_smooth/pallas_call | solution.py:493
  49.8 1.4 %copy.9 = f32[2,4,1536]{2,1,0:T(4,128)} copy(f32[2,4,1536]{2,1,0:T(4,128)} %bin_stack_smooth.1) | data formatting | bytes 98304

commit v5 on v3

--- a/solution.py
+++ b/solution.py
@@ -42,7 +42,7 @@
 
 def kernel(
     c, owner_ref, offset_ref, cell_ref, traces_hbm, slow_in, band_in, dip_ref, out_ref,
-    traces_ref, slow_ref, band_ref, send, send_meta, recv, recv_meta, slows, slow_parts, gather, picks, slow_rows, moved,
+    traces_ref, slow_ref, band_ref, packed, send, send_meta, recv, recv_meta, slows, slow_parts, gather, picks, slow_rows, moved,
     sums, sums_in, padded, lagged,
     t_sem, s_send, s_recv, m_send, m_recv, w_send, w_recv, z_send, z_recv, h_send, h_recv,
 ):
@@ -100,14 +100,15 @@
     band_ref[...] = band_in[...].reshape(1, samples)
     owner_row = owner_ref[...].reshape(1, count).astype(f32)
     turn = jnp.floor((owner_row + 0.5) * (1.0 / group))
-    base_row = (owner_row - turn * group) * rows + turn * cap
+    chunk_row = owner_row - turn * group
+    inner_row = turn * cap
     offset_row = offset_ref[...].astype(f32).reshape(1, count)
     cell_row = cell_ref[...].reshape(1, count).astype(f32) + 1.0
     owners = up_to(group * nz, 16)
     mine = jnp.where(iota((owners, count), 0).astype(f32) == owner_row, 1.0, 0.0)
     earlier = jnp.where(iota((count, count), 0) < iota((count, count), 1), 1.0, 0.0).astype(bf16)
     before = dot(mine.astype(bf16), earlier)
-    slot = base_row + jnp.sum(mine * before, axis=0, keepdims=True)
+    inner_row = inner_row + jnp.sum(mine * before, axis=0, keepdims=True)
     values = jnp.concatenate([offset_row, cell_row, jnp.zeros((14, count), f32)], axis=0).astype(bf16)
 
     def span_of(at, size):
@@ -122,53 +123,65 @@
             device_id=z_id(k), device_id_type=MESH,
         )
 
+    def chunk_of(k):
+        tx, ti = plane(k)
+        return tx * nil + ti
+
     def row_copy(k):
         return pltpu.make_async_remote_copy(
-            src_ref=send.at[k], dst_ref=recv.at[pl.ds(pl.multiple_of(k * rows, 16), rows), pl.ds(0, samples)],
+            src_ref=send.at[chunk_of(k)], dst_ref=recv.at[pl.ds(pl.multiple_of(k * rows, 16), rows), pl.ds(0, samples)],
             send_sem=s_send.at[k], recv_sem=s_recv.at[k], device_id=plane_id(k), device_id_type=MESH,
         )
 
     def meta_copy(k):
         return pltpu.make_async_remote_copy(
-            src_ref=send_meta.at[k], dst_ref=recv_meta.at[k],
+            src_ref=send_meta.at[chunk_of(k)], dst_ref=recv_meta.at[k],
             send_sem=m_send.at[k], recv_sem=m_recv.at[k], device_id=plane_id(k), device_id_type=MESH,
         )
 
     lax.fori_loop(1, nz, lambda k, _: (slow_copy(k).start(), 0)[1], 0)
 
-    def pack(k):
-        tx, ti = plane(k)
-        first = ((tx * nil + ti) * rows).astype(f32)
-        hot = jnp.where(iota((c.meta_rows, count), 0).astype(f32) + first == slot, 1.0, 0.0).astype(bf16)
-        chunk = dot(hot[:rows], traces_ref[...])
-        chunk = pltpu.roll(chunk, LANES // 2, 1).astype(bf16)
-        info = lax.dot_general(values, hot, NT_DIMS, preferred_element_type=f32).astype(bf16)
-        return chunk, info
+    def one_hot(step):
+        place = iota((group * step, count), 0).astype(f32)
+        return jnp.where(place == chunk_row * step + inner_row, 1.0, 0.0).astype(bf16)
+
+    info = lax.dot_general(values, one_hot(c.meta_rows), NT_DIMS, preferred_element_type=f32).astype(bf16)
+    for k in range(group):
+        send_meta[k] = info[:, k * c.meta_rows : (k + 1) * c.meta_rows]
+    traces_copy.wait()
+    packed[...] = dot(one_hot(rows), traces_ref[...])
+
+    def turn_chunk(k, _):
+        chunk = packed[pl.ds(pl.multiple_of(k * rows, 16), rows), :]
+        send[k] = pltpu.roll(chunk, LANES // 2, 1).astype(bf16)
+        return 0
+
+    lax.fori_loop(0, group, turn_chunk, 0)
 
     def send_one(k, _):
-        chunk, info = pack(k)
-        send[k] = chunk
-        send_meta[k] = info
         meta_copy(k).start()
         row_copy(k).start()
         return 0
 
-    traces_copy.wait()
     lax.fori_loop(1, group, send_one, 0)
-    chunk, info = pack(0)
-    recv[0:rows, 0:samples] = chunk
-    recv_meta[0] = info
+    recv[0:rows, 0:samples] = send[pl.ds(chunk_of(0), 1)][0]
+    recv_meta[0] = send_meta[pl.ds(chunk_of(0), 1)][0]
+
+    low = (LANES // 2 - BAND) // 16 * 16
+    high = up_to(LANES + LANES // 2 + BAND, 16)
 
     def make_gather(b, _):
+        gather[b, :low, :] = jnp.zeros((low, BAND * LANES), bf16)
+        gather[b, high:, :] = jnp.zeros((2 * LANES - high, BAND * LANES), bf16)
         start = pl.multiple_of(b * LANES, LANES)
         position = band_ref[:, pl.ds(start, LANES)] - start + LANES // 2
-        window = iota((2 * LANES, LANES), 0)
+        window = iota((high - low, LANES), 0) + low
         for pair in range(HALF):
             first = jnp.where(window == position + pair, 1.0, 0.0)
             last = jnp.where(window == position + (BAND - 1 - pair), 1.0, 0.0)
             at = pair * 2 * LANES
-            gather[b, :, at : at + LANES] = (first + last).astype(bf16)
-            gather[b, :, at + LANES : at + 2 * LANES] = ((first - last) * float(BAND - 1 - 2 * pair)).astype(bf16)
+            gather[b, low:high, at : at + LANES] = (first + last).astype(bf16)
+            gather[b, low:high, at + LANES : at + 2 * LANES] = ((first - last) * float(BAND - 1 - 2 * pair)).astype(bf16)
         return 0
 
     lax.fori_loop(0, blocks, make_gather, 0)
@@ -182,10 +195,6 @@
     slow_parts[3 * bins :, :] = jnp.zeros((bins, samples), bf16)
 
     sums[...] = jnp.zeros_like(sums)
-    batch = c.batch
-    batch_rows = batch * rows
-    tile = 32 if batch_rows % 32 == 0 else 16
-
     pieces = c.pieces
     per_piece = blocks // pieces
 
@@ -200,21 +209,21 @@
             device_id=z_id(k), device_id_type=MESH,
         )
 
-    def one_batch(i, last):
+    def one_batch(first, batch, last):
+        batch_rows = batch * rows
+        tile = 32 if batch_rows % 32 == 0 else 16
         for j in range(batch):
-            k = i * batch + j
-
-            @pl.when(k > 0)
-            def _():
+            k = first + j
+            if k > 0:
                 meta_copy(k).wait_recv()
                 row_copy(k).wait_recv()
 
-        span = pl.ds(pl.multiple_of(i * batch_rows, 16), batch_rows)
+        span = pl.ds(first * rows, batch_rows)
         recv[span, samples : samples + LANES] = recv[span, 0:LANES]
         same = jnp.where(iota((rows, c.meta_rows), 0) == iota((rows, c.meta_rows), 1), 1.0, 0.0).astype(bf16)
         columns = jnp.concatenate(
             [
-                lax.dot_general(same, recv_meta[i * batch + j], NT_DIMS, preferred_element_type=f32)
+                lax.dot_general(same, recv_meta[first + j], NT_DIMS, preferred_element_type=f32)
                 for j in range(batch)
             ],
             axis=0,
@@ -236,12 +245,12 @@
         head = pl.ds(0, LANES)
         sums[:, :, head] = sums[:, :, head] + jnp.broadcast_to(fold, (bins, LANES)).reshape(nz, cells, LANES)
         offset2 = jnp.broadcast_to(offset * offset, (batch_rows, LANES))
-        moved[2] = offset2
+        moved[2, :batch_rows] = offset2
 
         def fetch(b, at):
             start = pl.multiple_of(b * LANES, LANES)
-            picks[at] = dot(recv[span, pl.ds(start, 2 * LANES)], gather[b])
-            slow_rows[at] = dot(members, slow_parts[:, pl.ds(start, LANES)])
+            picks[at, :batch_rows] = dot(recv[span, pl.ds(start, 2 * LANES)], gather[b])
+            slow_rows[at, :batch_rows] = dot(members, slow_parts[:, pl.ds(start, LANES)])
 
         def one_block(b, at_slot):
             start = pl.multiple_of(b * LANES, LANES)
@@ -278,7 +287,7 @@
                 return 0
 
             lax.fori_loop(0, batch_rows // tile, one_tile, 0, unroll=True)
-            high, low = parts(moved[at_slot], 2)
+            high, low = parts(moved[at_slot, :batch_rows], 2)
             total = dot(turned, high) + dot(turned, low)
             after = pl.ds(pl.multiple_of(start + LANES, LANES), LANES)
             sums[:, :, after] = sums[:, :, after] + total.reshape(nz, cells, LANES)
@@ -301,8 +310,10 @@
             for k in range(1, nz):
                 sum_copy(k, p).start()
 
-    lax.fori_loop(0, group // batch - 1, lambda i, _: one_batch(i, False), 0)
-    one_batch(group // batch - 1, True)
+    first = 0
+    for batch in c.batches:
+        one_batch(first, batch, first + batch == group)
+        first += batch
 
     bx, by = c.bx, c.by
     wide = by + 2
@@ -430,13 +441,13 @@
     c.rows = up_to(c.nz * c.cap, 16)
     c.meta_rows = up_to(c.rows, LANES)
     c.bx, c.by = slowness.shape[:2]
-    c.batch = 2
+    c.batches = (c.group // 4, c.group // 2, c.group // 4)
     c.pieces = 3
     cells = c.bx * c.by
     bins = c.nz * cells
     samples = c.samples
     blocks = samples // LANES
-    batch_rows = c.batch * c.rows
+    batch_rows = max(c.batches) * c.rows
     lag_rows = up_to((c.bx + 2) * (c.by + 2), 8)
     dma = pltpu.SemaphoreType.DMA
     strip_count = 2 + 2 * c.bx + 4
@@ -452,6 +463,7 @@
             pltpu.VMEM((count, samples), bf16),
             pltpu.VMEM((cells, samples), f32),
             pltpu.VMEM((1, samples), jnp.int32),
+            pltpu.VMEM((c.group * c.rows, samples), f32),
             pltpu.VMEM((c.group, c.rows, samples), bf16),
             pltpu.VMEM((c.group, 16, c.meta_rows), bf16),
             pltpu.VMEM((c.group * c.rows, samples + LANES), bf16),

time: 47 us -> 47.9 us (1.019)
  Pallas kernels: 44.9 us -> 45.8 us
    pallas_call x1, Pallas kernels: 44.9 us -> 45.8 us  [body(): pl.pallas_call(functools.partial(kernel, c), out_shape=jax.ShapeDtypeStru...]
where the time goes in v5:
time: 47.9 us; the launch traced here: 47.3 us
  Pallas kernels  45.8 us (96%)
  local copies, waits for them, and re-layouts  1.42 us (3%)
    pallas_call x1, Pallas kernels, body(): pl.pallas_call(functools.partial(kernel, c), out_shape=jax.ShapeDtypeStru...  45.8 us
    unnamed x1, local copies, waits for them, and re-layouts  1.42 us

profile of v5, /device:TPU:0, one launch (start us, length us, event | category | flops | bytes accessed | tf_op | source)
XLA Modules:
  0.0 47.3 jit_solution(704084259852839500)
XLA Ops:
  0.0 45.8 %bin_stack_smooth.1 = f32[2,4,1536]{2,1,0:T(4,128)} custom-call(s32[512]{0:T(512)} %owner_ref.1, bf16[512]{0:T(512)(128)(2,1)} %offset_ref.1, s32[512]{0:T(512)} %cell_ref.1, bf16[512,1536]{1,0:T(8,128)(2,1)} %traces_hbm.1, f32[2,4,1536]{2,1,0:T(4,128)} %slow_in.1, s32[1536]{0:T(1024)} %band_in.1, s32[2,4,9]{2,1,0:T(4,128)} %bitcast.1), custom_call_target="tpu_custom_call" | custom-call | tf_op jit(solution)/shard_map/bin_stack_smooth/pallas_call | solution.py:454
  45.8 1.4 %copy.9 = f32[2,4,1536]{2,1,0:T(4,128)} copy(f32[2,4,1536]{2,1,0:T(4,128)} %bin_stack_smooth.1) | data formatting | bytes 98304

commit v6 on v3

--- a/solution.py
+++ b/solution.py
@@ -159,16 +159,21 @@
     recv[0:rows, 0:samples] = chunk
     recv_meta[0] = info
 
+    low = (LANES // 2 - BAND) // 16 * 16
+    high = up_to(LANES + LANES // 2 + BAND, 16)
+
     def make_gather(b, _):
+        gather[b, :low, :] = jnp.zeros((low, BAND * LANES), bf16)
+        gather[b, high:, :] = jnp.zeros((2 * LANES - high, BAND * LANES), bf16)
         start = pl.multiple_of(b * LANES, LANES)
         position = band_ref[:, pl.ds(start, LANES)] - start + LANES // 2
-        window = iota((2 * LANES, LANES), 0)
+        window = iota((high - low, LANES), 0) + low
         for pair in range(HALF):
             first = jnp.where(window == position + pair, 1.0, 0.0)
             last = jnp.where(window == position + (BAND - 1 - pair), 1.0, 0.0)
             at = pair * 2 * LANES
-            gather[b, :, at : at + LANES] = (first + last).astype(bf16)
-            gather[b, :, at + LANES : at + 2 * LANES] = ((first - last) * float(BAND - 1 - 2 * pair)).astype(bf16)
+            gather[b, low:high, at : at + LANES] = (first + last).astype(bf16)
+            gather[b, low:high, at + LANES : at + 2 * LANES] = ((first - last) * float(BAND - 1 - 2 * pair)).astype(bf16)
         return 0
 
     lax.fori_loop(0, blocks, make_gather, 0)
@@ -184,7 +189,7 @@
     sums[...] = jnp.zeros_like(sums)
     batch = c.batch
     batch_rows = batch * rows
-    tile = 32 if batch_rows % 32 == 0 else 16
+    tile = 16
 
     pieces = c.pieces
     per_piece = blocks // pieces
@@ -386,7 +391,7 @@
         shifted = whole if lag == 0 else pltpu.roll(whole, (-lag) % samples, 1)
         inside = (time + lag >= 0) & (time + lag < samples)
         lagged[i * lag_rows : (i + 1) * lag_rows, :] = jnp.where(inside, shifted, 0.0)
-    result = sum(dot(weights, piece) for piece in parts(lagged[...], 3))
+    result = sum(dot(weights, piece) for piece in parts(lagged[...], 2))
     for row in range(bx):
         out_ref[row] = result[row * by : (row + 1) * by, :]
 

time: 47 us -> 46.7 us (level)
  no operation moved by 1% of the time
where the time goes in v6:
time: 46.7 us; the launch traced here: 46.3 us
  Pallas kernels  44.8 us (96%)
  local copies, waits for them, and re-layouts  1.42 us (3%)
    pallas_call x1, Pallas kernels, body(): pl.pallas_call(functools.partial(kernel, c), out_shape=jax.ShapeDtypeStru...  44.8 us
    unnamed x1, local copies, waits for them, and re-layouts  1.42 us

profile of v6, /device:TPU:0, one launch (start us, length us, event | category | flops | bytes accessed | tf_op | source)
XLA Modules:
  0.0 46.3 jit_solution(11763923109406063587)
XLA Ops:
  0.0 44.8 %bin_stack_smooth.1 = f32[2,4,1536]{2,1,0:T(4,128)} custom-call(s32[512]{0:T(512)} %owner_ref.1, bf16[512]{0:T(512)(128)(2,1)} %offset_ref.1, s32[512]{0:T(512)} %cell_ref.1, bf16[512,1536]{1,0:T(8,128)(2,1)} %traces_hbm.1, f32[2,4,1536]{2,1,0:T(4,128)} %slow_in.1, s32[1536]{0:T(1024)} %band_in.1, s32[2,4,9]{2,1,0:T(4,128)} %bitcast.1), custom_call_target="tpu_custom_call" | custom-call | tf_op jit(solution)/shard_map/bin_stack_smooth/pallas_call | solution.py:448
  44.8 1.4 %copy.9 = f32[2,4,1536]{2,1,0:T(4,128)} copy(f32[2,4,1536]{2,1,0:T(4,128)} %bin_stack_smooth.1) | data formatting | bytes 98304
